TPU v7x, 256 devices: a whole 4x4x8 slice. The times are simulated.
256 devices in a mesh: dp: 16 (over z, x_lo), tensor: 16 (over x_hi, y, core).
Axes of the slice: x: 4 (x_hi: 2, x_lo: 2; x = x_hi * 2 + x_lo), y: 4, z: 8, core: 2. Of those that a mesh axis runs over, the one named last changes fastest.
Arguments:
- residual_in: bfloat16 [8192, 5120], P('dp'), may hold values from -6 to 6
- layernorm_gain: float32 [5120], replicated, may hold values from 0.2 to 8, as said below
- layernorm_bias: float32 [5120], replicated, may hold values from -3 to 3
- qkv_weight: bfloat16 [3, 5120, 4096], P(None, 'dp', 'tensor'), may hold values from -2.5 to 2.5, as said below
- out_weight: bfloat16 [4096, 5120], P('tensor', 'dp'), may hold values from -0.09375 to 0.09375
- encoder: bfloat16 [5120, 640], P('dp'), may hold values from -0.078125 to 0.078125
- decoder: bfloat16 [640, 5120], P(None, 'tensor'), may hold values from -0.25 to 0.25
- grad_output: bfloat16 [8192, 5120], P('dp', 'tensor'), may hold values from -6 to 6
Outputs:
- residual_out: bfloat16 [8192, 5120], P('dp', 'tensor')
- grad_input: bfloat16 [8192, 5120], P('dp', 'tensor')
- grad_qkv: float32 [3, 5120, 4096], P(None, 'dp', 'tensor')
- grad_out_weight: float32 [4096, 5120], P('tensor', 'dp')
- grad_gain: float32 [5120], P('tensor')
- grad_bias: float32 [5120], P('tensor')
Inputs may be any that keep to these rules, and one draw needn't show every extreme that they name: `qkv_weight`: projections to queries, keys and values; entries of order 1 / sqrt(5120) or larger. `layernorm_gain`: positive gains.
All inputs are finite; a program needn't handle non-finite values.
Results may differ from a plain program's by a relative error of at most 0.035.
Values may be sent and summed in bfloat16 or wider, within the bound.
A program may use at most 192 MiB of HBM per device.

v0:
```python
import jax
import jax.numpy as jnp
from jax import lax
from jax.sharding import PartitionSpec as P

HDIM = 128


EPS = 1e-05
HIGH = lax.Precision.HIGHEST


def attention_core(qkv, head_size):
    seq = qkv.shape[0]
    feature_width = qkv.shape[2]
    heads = feature_width // head_size
    split = qkv.reshape(seq, 3, heads, head_size)
    query = split[:, 0]
    keys = split[:, 1]
    values = split[:, 2]
    scores = jnp.einsum("qhd,khd->hqk", query, keys, preferred_element_type=jnp.float32) / jnp.sqrt(
        jnp.float32(head_size)
    )
    rows = lax.broadcasted_iota(jnp.int32, (seq, seq), 0)
    column_list = lax.broadcasted_iota(jnp.int32, (seq, seq), 1)
    scores = jnp.where((column_list <= rows)[None], scores, jnp.float32(-1e30))
    top = jnp.max(scores, axis=2, keepdims=True)
    expo = jnp.exp(scores - top)
    probs = expo / jnp.sum(expo, axis=2, keepdims=True)
    mixed = jnp.einsum(
        "hqk,khd->qhd", probs.astype(jnp.bfloat16), values, preferred_element_type=jnp.float32
    )
    return mixed.reshape(seq, feature_width).astype(jnp.bfloat16)


def local(
    residual_in,
    layernorm_gain,
    layernorm_bias,
    qkv_weight,
    out_weight,
    encoder,
    decoder,
    grad_output,
):
    seq, feature_width = residual_in.shape
    column_list = decoder.shape[1]
    start_offset = lax.axis_index("tensor") * column_list
    replicas = lax.axis_size("dp")
    input_float = residual_in.astype(jnp.float32)
    row_mean = jnp.mean(input_float, axis=1, keepdims=True)
    var = jnp.mean((input_float - row_mean) ** 2, axis=1, keepdims=True)
    inverse_deviation = lax.rsqrt(var + EPS)
    centered_input = (input_float - row_mean) * inverse_deviation
    normalized_rows = (centered_input * layernorm_gain + layernorm_bias).astype(jnp.bfloat16)
    weights = lax.all_gather(qkv_weight, "dp", axis=1, tiled=True)
    qkv = jnp.einsum(
        "td,jdq->tjq", normalized_rows, weights, preferred_element_type=jnp.float32
    ).astype(jnp.bfloat16)
    attn = attention_core(qkv, HDIM)
    folded = lax.psum(
        jnp.dot(out_weight, encoder, preferred_element_type=jnp.float32).astype(jnp.bfloat16), "dp"
    ).astype(jnp.float32)
    code_part = jnp.dot(attn.astype(jnp.float32), folded, precision=HIGH)
    code = lax.psum(code_part.astype(jnp.bfloat16), "tensor")
    decoded = jnp.dot(code, decoder, preferred_element_type=jnp.float32)
    x_cols = lax.dynamic_slice_in_dim(input_float, start_offset, column_list, 1)
    residual_out = (x_cols + decoded).astype(jnp.bfloat16)
    code_grad = lax.psum(
        jnp.dot(grad_output, decoder.T, preferred_element_type=jnp.float32).astype(jnp.bfloat16),
        "tensor",
    ).astype(jnp.float32)
    attn_grad = jnp.dot(code_grad, folded.T, precision=HIGH).astype(jnp.bfloat16)
    mixing = jnp.dot(attn.astype(jnp.float32).T, code_grad, precision=HIGH)
    _, pullback = jax.vjp(lambda t: attention_core(t, HDIM), qkv)
    qkv_grad = pullback(attn_grad)[0]
    input_part = jnp.einsum("tjq,jdq->td", qkv_grad, weights, preferred_element_type=jnp.float32)
    layernorm_gradient = lax.psum_scatter(
        input_part.astype(jnp.bfloat16), "tensor", scatter_dimension=1, tiled=True
    ).astype(jnp.float32)
    centered_columns = lax.dynamic_slice_in_dim(centered_input, start_offset, column_list, 1)
    gain_cols = lax.dynamic_slice_in_dim(layernorm_gain, start_offset, column_list, 0)
    scaled_rows = layernorm_gradient * gain_cols
    leading_part, trailing_part = lax.psum(
        (jnp.sum(scaled_rows, axis=1), jnp.sum(scaled_rows * centered_columns, axis=1)), "tensor"
    )
    grad_input = (
        grad_output.astype(jnp.float32)
        + inverse_deviation
        * (
            scaled_rows
            - leading_part[:, None] / feature_width
            - centered_columns * trailing_part[:, None] / feature_width
        )
    ).astype(jnp.bfloat16)
    gain_product = jnp.sum(layernorm_gradient * centered_columns, axis=0)
    bias_term = jnp.sum(layernorm_gradient, axis=0)
    mixing, gain_product, bias_term = (
        lax.psum(mixing.astype(jnp.bfloat16), "dp").astype(jnp.float32),
        lax.psum(gain_product.astype(jnp.bfloat16), "dp").astype(jnp.float32),
        lax.psum(bias_term.astype(jnp.bfloat16), "dp").astype(jnp.float32),
    )
    grad_out_weight = jnp.dot(mixing, encoder.astype(jnp.float32).T, precision=HIGH) / replicas
    summed = lax.psum_scatter(
        jnp.einsum(
            "td,tjq->djq", normalized_rows, qkv_grad, preferred_element_type=jnp.float32
        ).astype(jnp.bfloat16),
        "dp",
        scatter_dimension=0,
        tiled=True,
    ).astype(jnp.float32)
    grad_qkv = jnp.transpose(summed, (1, 0, 2)) / replicas
    return (
        residual_out,
        grad_input,
        grad_qkv,
        grad_out_weight,
        gain_product / replicas,
        bias_term / replicas,
    )


def solution(mesh):
    in_specs = (
        P("dp", None),
        P(),
        P(),
        P(None, "dp", "tensor"),
        P("tensor", "dp"),
        P("dp", None),
        P(None, "tensor"),
        P("dp", "tensor"),
    )
    out_specs = (
        P("dp", "tensor"),
        P("dp", "tensor"),
        P(None, "dp", "tensor"),
        P("tensor", "dp"),
        P("tensor"),
        P("tensor"),
    )
    return jax.shard_map(local, mesh=mesh, in_specs=in_specs, out_specs=out_specs, check_vma=False)
```

profile of v0, /device:TPU:1, one launch (start us, length us, event | category | flops | bytes accessed | tf_op | source)
XLA Modules:
  0.0 900.5 jit_solution(5387500773847944475)
XLA Ops:
  8.0 2.2 convolution_convert_fusion.6
  10.3 8.0 copy.14
  18.4 3.4 convert_reduce_fusion
  25.3 159.9 %all-gather.2.cloned.1.call-done = bf16[3,5120,256]{2,1,0:T(8,128)(2,1)} async-done(((bf16[3,320,256]{2,1,0:T(8,128)(2,1)}), bf16[3,5120,256]{2,1,0:T(8,128)(2,1)}) %all-gather.2.cloned.1.call-update) | async-done | bytes 7864336 | tf_op jit(solution)/shard_map/all_gather | solution.py:56
  185.3 9.6 %convolution_convert_fusion.2 = bf16[512,3,256]{0,2,1:T(8,128)(2,1)S(1)} fusion(bf16[3,5120,256]{2,1,0:T(8,128)(2,1)} %all-gather.2.cloned.1.call-done, f32[5120]{0:T(1024)S(1)} %copy-done.22, f32[5120]{0:T(1024)S(1)} %copy-done.20, f32[512]{0:T(512)S(1)} %add_rsqrt_fusion, f32[512]{0:T(512)S(1)} %broadcast_multiply_fusion.1, bf16[512,5120]{0,1:T(8,128)(2,1)} %copy.14), kind=kOutput, calls=%fused_computation.19 | convolution fusion | flops 4042653696 | bytes 13938688 | tf_op jit(solution)/shard_map/td,jdq->tjq/dot_general | solution.py:57
  197.9 117.2 %all-reduce.10.cloned.1.call-done = bf16[256,640]{1,0:T(8,128)(2,1)} async-done(((bf16[256,640]{1,0:T(8,128)(2,1)}), bf16[256,640]{1,0:T(8,128)(2,1)}) %all-reduce.10.cloned.1.call-update) | async-done | bytes 327696 | tf_op jit(solution)/shard_map/psum | solution.py:61
  315.1 2.3 convolution_convert_fusion.4
  318.9 155.4 %all-reduce.14.cloned.1.call-done = (bf16[512,640]{1,0:T(8,128)(2,1)}, bf16[512,640]{1,0:T(8,128)(2,1)}) async-done(((bf16[512,640]{1,0:T(8,128)(2,1)}, bf16[512,640]{1,0:T(8,128)(2,1)}), (bf16[512,640]{1,0:T(8,128)(2,1)}, bf16[512,640]{1,0:T(8,128)(2,1)})) %all-reduce.14.cloned.1.call-update) | async-done | bytes 1310736 | tf_op jit(solution)/shard_map/psum | solution.py:65
  474.3 2.3 convolution_convert_fusion.5
  476.6 1.6 convolution_convert_fusion.9
  483.8 9.2 %bitcast_convert_fusion = bf16[512,5120]{0,1:T(8,128)(2,1)} fusion(bf16[3,5120,256]{2,1,0:T(8,128)(2,1)} %all-gather.2.cloned.1.call-done, bf16[512,3,256]{0,2,1:T(8,128)(2,1)S(1)} %bitcast.77), kind=kOutput, calls=%fused_computation | convolution fusion | flops 4029153280 | bytes 13893632 | tf_op jit(solution)/shard_map/tjq,jdq->td/dot_general | solution.py:77
  493.8 9.4 %convolution_convert_fusion = bf16[5120,3,256]{2,0,1:T(8,128)(2,1)} fusion(bf16[512,3,256]{0,2,1:T(8,128)(2,1)S(1)} %bitcast.78, f32[5120]{0:T(1024)S(1)} %copy-done.23, f32[5120]{0:T(1024)S(1)} %copy-done.21, f32[512]{0:T(512)S(1)} %copy-done.16, f32[512]{0:T(512)S(1)} %copy-done.18, bf16[512,5120]{0,1:T(8,128)(2,1)} %copy.14), kind=kOutput, calls=%fused_computation.4 | convolution fusion | flops 4046192640 | bytes 13938688 | tf_op jit(solution)/shard_map/td,tjq->djq/dot_general | solution.py:105
  503.3 7.8 convert_element_type.102
  511.2 8.1 subtract_multiply_fusion
  519.3 2.3 fusion.10
  521.7 88.8 %all-reduce.12.cloned.1.call-done = bf16[256,640]{1,0:T(8,128)(2,1)} async-done(((bf16[256,640]{1,0:T(8,128)(2,1)}), bf16[256,640]{1,0:T(8,128)(2,1)}) %all-reduce.12.cloned.1.call-update) | async-done | bytes 327696 | tf_op jit(solution)/shard_map/psum | solution.py:99
  610.5 2.0 convolution_multiply_fusion
  612.5 103.0 %reduce-scatter.3.cloned.1.call-done = bf16[512,320]{0,1:T(8,128)(2,1)} async-done(((bf16[512,5120]{0,1:T(8,128)(2,1)}), bf16[512,320]{0,1:T(8,128)(2,1)}) %reduce-scatter.3.cloned.1.call-update) | async-done | bytes 327696 | tf_op jit(solution)/shard_map/reduce_scatter | solution.py:78
  716.6 1.5 fusion.32
  718.1 28.6 %all-reduce.5 = (bf16[320]{0:T(512)(128)(2,1)S(1)}, bf16[320]{0:T(512)(128)(2,1)S(1)}) all-reduce(bf16[320]{0:T(512)(128)(2,1)S(1)} %get-tuple-element.6, bf16[320]{0:T(512)(128)(2,1)S(1)} %reduce_sum.114), channel_id=1, replica_groups=mesh['dp'=16,'tensor'=16] {'dp'}, use_global_device_ids=true, to_apply=%region_18.19 | all-reduce | flops 640 | bytes 2560 | tf_op jit(solution)/shard_map/psum | solution.py:100
  746.7 52.1 %all-reduce.3 = (f32[512]{0:T(512)S(1)}, f32[512]{0:T(512)S(1)}) all-reduce(f32[512]{0:T(512)S(1)} %get-tuple-element.7, f32[512]{0:T(512)S(1)} %get-tuple-element.8), channel_id=1, replica_groups=mesh['dp'=16,'tensor'=16] {'tensor'}, use_global_device_ids=true, to_apply=%region_14.15 | all-reduce | flops 1024 | bytes 8192 | tf_op jit(solution)/shard_map/psum | solution.py:84
  799.3 2.2 fusion.30
  801.5 90.1 %reduce-scatter.5.cloned.1.call-done = bf16[320,3,256]{2,0,1:T(8,128)(2,1)} async-done(((bf16[5120,3,256]{2,0,1:T(8,128)(2,1)}), bf16[320,3,256]{2,0,1:T(8,128)(2,1)}) %reduce-scatter.5.cloned.1.call-update) | async-done | bytes 491536 | tf_op jit(solution)/shard_map/reduce_scatter | solution.py:104
  891.6 2.1 multiply_bitcast_fusion
  (82 shorter events, 16.9 us)
Async XLA Ops:
  7.2 16.7 %copy-start = (bf16[640,320]{0,1:T(8,128)(2,1)S(1)}, bf16[640,320]{0,1:T(8,128)(2,1)}, u32[]{:S(2)}) copy-start(bf16[640,320]{0,1:T(8,128)(2,1)} %param.14) | copy-start | bytes 1228804
  7.2 178.1 %all-gather.2.cloned.1.call-start = ((), (), s32[]{:S(2)}) async-start(), calls=%async_computation.2 | async-start | bytes 8355840 | tf_op jit(solution)/shard_map/all_gather | solution.py:56
  7.9 307.2 %all-reduce.10.cloned.1.call-start = ((), (), s32[]{:S(2)}) async-start(), calls=%async_computation.3 | async-start | bytes 655360 | tf_op jit(solution)/shard_map/psum | solution.py:61
  10.2 464.1 %all-reduce.14.cloned.1.call-start = ((), (), s32[]{:S(2)}) async-start(), calls=%async_computation.7 | async-start | bytes 2621440 | tf_op jit(solution)/shard_map/psum | solution.py:65
  10.3 184.6 %copy-start.9 = (pred[512,512]{0,1:T(8,128)(4,1)}, pred[512,512]{0,1:T(8,128)(4,1)S(1)}, u32[]{:S(2)}) copy-start(pred[512,512]{0,1:T(8,128)(4,1)S(1)} %iota_compare_fusion) | copy-start | bytes 786436
  18.4 4.0 copy-start.1
  22.4 162.9 %copy-start.17 = (f32[512]{0:T(512)}, f32[512]{0:T(512)S(1)}, u32[]{:S(2)}) copy-start(f32[512]{0:T(512)S(1)} %broadcast_multiply_fusion.1) | copy-start | bytes 6148
  22.4 1.4 copy-start.3
  22.4 162.9 %copy-start.20 = (f32[5120]{0:T(1024)S(1)}, f32[5120]{0:T(1024)}, u32[]{:S(2)}) copy-start(f32[5120]{0:T(1024)} %param.9) | copy-start | bytes 61444
  22.4 162.9 %copy-start.22 = (f32[5120]{0:T(1024)S(1)}, f32[5120]{0:T(1024)}, u32[]{:S(2)}) copy-start(f32[5120]{0:T(1024)} %param.10) | copy-start | bytes 61444
  23.9 171.1 %copy-start.15 = (f32[512]{0:T(512)}, f32[512]{0:T(512)S(1)}, u32[]{:S(2)}) copy-start(f32[512]{0:T(512)S(1)} %add_rsqrt_fusion) | copy-start | bytes 6148
  194.9 1.9 copy-start.7
  195.6 1.3 copy-start.13
  317.4 293.1 %all-reduce.12.cloned.1.call-start = ((), (), s32[]{:S(2)}) async-start(), calls=%async_computation.6 | async-start | bytes 655360 | tf_op jit(solution)/shard_map/psum | solution.py:99
  476.6 2.8 copy-start.8
  476.6 2.8 copy-start.14
  476.6 2.8 copy-start.19
  480.1 1.0 copy-start.10
  482.4 1.4 copy-start.5
  483.7 231.8 %reduce-scatter.3.cloned.1.call-start = ((), (), s32[]{:S(2)}) async-start(), calls=%async_computation.4 | async-start | bytes 5570560 | tf_op jit(solution)/shard_map/reduce_scatter | solution.py:78
  493.1 398.5 %reduce-scatter.5.cloned.1.call-start = ((), (), s32[]{:S(2)}) async-start(), calls=%async_computation.5 | async-start | bytes 8355840 | tf_op jit(solution)/shard_map/reduce_scatter | solution.py:104
  511.2 8.2 copy-start.6
  519.3 91.2 %copy-start.2 = (bf16[320,640]{1,0:T(8,128)(2,1)S(1)}, bf16[320,640]{1,0:T(8,128)(2,1)}, u32[]{:S(2)}) copy-start(bf16[320,640]{1,0:T(8,128)(2,1)} %param.13) | copy-start | bytes 1228804
  519.3 280.0 %copy-start.4 = (bf16[512,320]{0,1:T(8,128)(2,1)S(1)}, bf16[512,320]{0,1:T(8,128)(2,1)}, u32[]{:S(2)}) copy-start(bf16[512,320]{0,1:T(8,128)(2,1)} %param.15) | copy-start | bytes 983044
  (6 other events, 4.2 us)
Sparse Core Ops, SparseCore 0:
  9.8 175.4 all-gather.1
  188.5 126.5 all-reduce.9
  318.0 156.2 all-reduce.13
  483.8 126.6 all-reduce.11
  614.7 100.7 reduce-scatter.2
  717.9 173.6 reduce-scatter.4
where the time goes:
time: 901 us; the launch traced here: 900 us
  waiting for transfers between devices  715 us (79%)
  blocking collectives  80.7 us (9%)
  matrix products  48.5 us (5%)
  other arithmetic  31.3 us (3%)
  between operations  14.3 us (2%)
  local copies, waits for them, and re-layouts  9.91 us (1%)
    all_gather x1, waiting for transfers between devices, local(): weights = lax.all_gather(qkv_weight, 'dp', axis=1, tiled=True)  160 us
    psum x1, waiting for transfers between devices, local(): code = lax.psum(code_part.astype(jnp.bfloat16), 'tensor')  155 us
    psum x1, waiting for transfers between devices, local(): lax.psum(jnp.dot(out_weight, encoder, preferred_element_type=jnp.float32)...  117 us
    reduce_scatter x1, waiting for transfers between devices, local(): lax.psum_scatter(input_part.astype(jnp.bfloat16), 'tensor', scatter_dimen...  103 us
    reduce_scatter x1, waiting for transfers between devices, local(): lax.psum_scatter(jnp.einsum('td,tjq->djq', normalized_rows, qkv_grad, pre...  90.1 us
    psum x1, waiting for transfers between devices, local(): lax.psum(mixing.astype(jnp.bfloat16), 'dp').astype(jnp.float32)  88.8 us
    psum x1, blocking collectives, local(): lax.psum((jnp.sum(scaled_rows, axis=1), jnp.sum(scaled_rows * centered_co...  52.1 us
    psum x1, blocking collectives, local(): lax.psum(gain_product.astype(jnp.bfloat16), 'dp').astype(jnp.float32)  28.6 us
  transfers between devices with their start and end apart: 6, of which 6 were waited for; matrix products, arithmetic and copies ran while one was open for 8% of the time, Pallas kernels for 0%

commit v1 on v0

v1 whole, which is shorter than its diff:
```python
import functools

import jax
import jax.numpy as jnp
from jax import lax
from jax.experimental import pallas as pl
from jax.experimental.pallas import tpu as pltpu
from jax.sharding import PartitionSpec as P

HDIM = 128
EPS = 1e-05
MESH = pl.DeviceIdType.MESH
F32, BF = jnp.float32, jnp.bfloat16

NZ, NY, NQ, NR = 8, 4, 8, 16
SEQ, D, C, W3 = 512, 5120, 640, 768
BLK = 320
SLAB = 640
LR = 192
RB = SLAB - LR
CH = RB // 2
BR = BLK - LR


def rem(a, n):
    return lax.rem(a, n)


def rows(start, size):
    return pl.ds(pl.multiple_of(start, 16), size)


def dot(a, b):
    return lax.dot_general(a, b, (((1,), (0,)), ((), ())), preferred_element_type=F32)


def dot_tn(a, b):
    return lax.dot_general(a, b, (((0,), (0,)), ((), ())), preferred_element_type=F32)


def remote(src, dst, ssem, rsem, **device):
    return pltpu.make_async_remote_copy(
        src_ref=src, dst_ref=dst, send_sem=ssem, recv_sem=rsem, device_id=device, device_id_type=MESH
    )


def enter():
    barrier = pltpu.get_barrier_semaphore()
    for axis in ("dp", "tensor"):
        me = lax.axis_index(axis)
        for k in range(1, NR):
            pl.semaphore_signal(barrier, inc=1, device_id={axis: rem(me + k, NR)}, device_id_type=MESH)
    pl.semaphore_wait(barrier, 2 * (NR - 1))


class Sum:
    def __init__(self, axis, part, got, half, ring, out, ssem, rsem):
        self.axis, self.part, self.got, self.half, self.ring, self.out = axis, part, got, half, ring, out
        self.ssem, self.rsem = ssem, rsem
        index = lax.axis_index(axis)
        self.a, self.q = rem(index, 2), index // 2
        self.h = part.shape[0] // 2
        self.b = self.h // NQ
        self.sent = []

    def pair(self):
        return {self.axis: self.q * 2 + 1 - self.a}

    def peer(self, k):
        return {self.axis: rem(self.q + k, NQ) * 2 + self.a}

    def go(self, copy):
        copy.start()
        self.sent.append(copy)

    def first(self):
        src = self.part.at[rows((1 - self.a) * self.h, self.h), :]
        self.go(remote(src, self.got, self.ssem.at[0], self.rsem.at[0], **self.pair()))

    def second(self):
        remote(self.got, self.got, self.ssem.at[0], self.rsem.at[0], **self.pair()).wait_recv()
        mine = self.part[rows(self.a * self.h, self.h), :].astype(F32)
        self.half[...] = (mine + self.got[...].astype(F32)).astype(BF)
        for k in range(1, NQ):
            to = rem(self.q + k, NQ)
            self.go(
                remote(
                    self.half.at[rows(to * self.b, self.b), :],
                    self.ring.at[self.q],
                    self.ssem.at[k],
                    self.rsem.at[k],
                    **self.peer(k),
                )
            )

    def third(self):
        total = self.half[rows(self.q * self.b, self.b), :].astype(F32)
        for k in range(1, NQ):
            source = rem(self.q + NQ - k, NQ)
            slot = self.ring.at[source]
            remote(slot, slot, self.ssem.at[k], self.rsem.at[k], **self.peer(k)).wait_recv()
            total = total + self.ring[source].astype(F32)
        here = rows(self.a * self.h + self.q * self.b, self.b)
        self.out[here, :] = total.astype(BF)
        for k in range(1, NQ):
            piece = self.out.at[here, :]
            self.go(remote(piece, piece, self.ssem.at[7 + k], self.rsem.at[7 + k], **self.peer(k)))

    def fourth(self):
        for k in range(1, NQ):
            source = rem(self.q + NQ - k, NQ)
            piece = self.out.at[rows(self.a * self.h + source * self.b, self.b), :]
            remote(piece, piece, self.ssem.at[7 + k], self.rsem.at[7 + k], **self.peer(k)).wait_recv()
        mine = self.out.at[rows(self.a * self.h, self.h), :]
        self.go(remote(mine, mine, self.ssem.at[15], self.rsem.at[15], **self.pair()))

    def last(self):
        other = self.out.at[rows((1 - self.a) * self.h, self.h), :]
        remote(other, other, self.ssem.at[15], self.rsem.at[15], **self.pair()).wait_recv()

    def drain(self):
        for copy in self.sent:
            copy.wait_send()


def sum_scratch(r):
    h = r // 2
    return [
        pltpu.VMEM((h, C), BF),
        pltpu.VMEM((h, C), BF),
        pltpu.VMEM((NQ, h // NQ, C), BF),
        pltpu.SemaphoreType.DMA((16,)),
        pltpu.SemaphoreType.DMA((16,)),
    ]


def forward_kernel(
    x, gain, bias, w_in, owt, enc, dect, got,
    qkv, w_out, nt_out, mu, rstd, code_grad, folded,
    w, norm, normt, acc, cg_part, fo_part,
    t_got, t_half, t_ring, t_ss, t_rs,
    d_got, d_half, d_ring, d_ss, d_rs,
    a_ss, a_rs, b_ss, b_rs, c_ss, c_rs, loc, outs,
):
    dp = lax.axis_index("dp")
    z, xl = dp // 2, rem(dp, 2)
    up, down = rem(z + 1, NZ) * 2 + xl, rem(z + NZ - 1, NZ) * 2 + xl
    other = z * 2 + 1 - xl
    sent = []

    def go(copy):
        copy.start()
        sent.append(copy)

    def block(zs, offset, size):
        return w.at[:, rows(zs * SLAB + offset, size), :]

    own = BLK * xl
    shared = BLK - BR * xl
    crossing = RB * xl
    incoming = RB * (1 - xl)

    enter()
    mine = pltpu.make_async_copy(w_in, block(z, own, BLK), loc)
    mine.start()
    first = LR * (1 - xl)
    go(remote(w_in.at[:, rows(first, BR), :], block(z, own + first, BR), b_ss.at[0], b_rs.at[0], dp=other))
    for way, to in ((0, up), (1, down)):
        go(remote(w_in, block(z, own, BLK), a_ss.at[way, 0], a_rs.at[way, 0], dp=to))
    go(remote(w_in.at[:, rows(BR * xl, LR), :], block(z, crossing, LR), c_ss.at[0], c_rs.at[0], dp=other))

    cg_part[...] = dot_tn(got[...], dect[...]).astype(BF)
    sum_t = Sum("tensor", cg_part, t_got, t_half, t_ring, code_grad, t_ss, t_rs)
    sum_t.first()
    fo_part[...] = dot_tn(owt[...], enc[...]).astype(BF)
    sum_d = Sum("dp", fo_part, d_got, d_half, d_ring, folded, d_ss, d_rs)
    sum_d.first()

    piece = block(z, shared, BR)
    remote(piece, piece, b_ss.at[0], b_rs.at[0], dp=other).wait_recv()
    for way, to in ((0, up), (1, down)):
        go(remote(piece, piece, b_ss.at[1 + way * 4], b_rs.at[1 + way * 4], dp=to))

    @pl.loop(0, SEQ // 16)
    def _(i):
        here = rows(i * 16, 16)
        v = x[here, :].astype(F32)
        mean = jnp.sum(v, axis=1, keepdims=True) * (1.0 / D)
        v = v - mean
        var = jnp.sum(v * v, axis=1, keepdims=True) * (1.0 / D)
        scale = lax.rsqrt(var + EPS)
        mu[here, :] = mean
        rstd[here, :] = scale
        v = (v * scale * gain[...] + bias[...]).astype(BF)
        for s in range(NZ):
            norm[s, here, :] = v[:, s * SLAB : (s + 1) * SLAB]

    def step(s):
        for way, to, zs in ((0, up, rem(z + NZ - s, NZ)), (1, down, rem(z + s, NZ))):
            part = block(zs, own, BLK)
            remote(part, part, a_ss.at[way, s - 1], a_rs.at[way, s - 1], dp=to).wait_recv()
            if s == 3:
                part = block(zs, own + way * (BLK // 2), BLK // 2)
            go(remote(part, part, a_ss.at[way, s], a_rs.at[way, s], dp=to))
            part = block(zs, crossing, LR)
            k = s + way * 3
            go(remote(part, part, c_ss.at[k], c_rs.at[k], dp=other))
        for way, to, zs in ((0, up, rem(z + NZ - s, NZ)), (1, down, rem(z + s, NZ))):
            part = block(zs, shared, BR)
            k = s + way * 4
            remote(part, part, b_ss.at[k], b_rs.at[k], dp=to).wait_recv()
            if s == 3:
                part = block(zs, shared + way * (BR // 2), BR // 2)
            go(remote(part, part, b_ss.at[k + 1], b_rs.at[k + 1], dp=to))

    def use(zs, k, begin=False):
        part = block(zs, incoming, LR)
        remote(part, part, c_ss.at[k], c_rs.at[k], dp=other).wait_recv()
        whole = block(zs, 0, SLAB)
        leaves.append(pltpu.make_async_copy(whole, w_out.at[:, rows(zs * SLAB, SLAB), :], outs.at[k]))
        leaves[-1].start()

        @pl.loop(0, 2)
        def _(i):
            here = rows(i * 256, 256)
            a = norm[zs, here, :]
            for j in range(3):
                cols = slice(j * 256, (j + 1) * 256)
                term = dot(a, w[j, rows(zs * SLAB, SLAB), :])
                if begin:
                    acc[here, cols] = term
                else:
                    acc[here, cols] += term

        @pl.loop(0, 4)
        def _(i):
            here = pl.ds(pl.multiple_of(i * 128, 128), 128)
            normt[zs, :, here] = norm[zs, here, :].T

        leaves.append(pltpu.make_async_copy(normt.at[zs], nt_out.at[zs], outs.at[8 + k]))
        leaves[-1].start()

    leaves = []
    sum_t.second()
    sum_d.second()
    step(1)
    mine.wait()
    use(z, 0, True)
    sum_t.third()
    sum_d.third()
    step(2)
    use(rem(z + NZ - 1, NZ), 1)
    use(rem(z + 1, NZ), 4)
    sum_t.fourth()
    sum_d.fourth()
    step(3)
    use(rem(z + NZ - 2, NZ), 2)
    use(rem(z + 2, NZ), 5)
    z4 = rem(z + 4, NZ)
    for way, to in ((0, up), (1, down)):
        part = block(z4, own + way * (BLK // 2), BLK // 2)
        remote(part, part, a_ss.at[way, 3], a_rs.at[way, 3], dp=to).wait_recv()
    part = block(z4, crossing, LR)
    go(remote(part, part, c_ss.at[7], c_rs.at[7], dp=other))
    use(rem(z + NZ - 3, NZ), 3)
    use(rem(z + 3, NZ), 6)
    for way, to in ((0, up), (1, down)):
        part = block(z4, shared + way * (BR // 2), BR // 2)
        remote(part, part, b_ss.at[4 + way * 4], b_rs.at[4 + way * 4], dp=to).wait_recv()
    use(z4, 7)
    qkv[...] = acc[...].astype(BF)
    sum_t.last()
    sum_d.last()
    sum_t.drain()
    sum_d.drain()
    for copy in sent:
        copy.wait_send()
    for copy in leaves:
        copy.wait()


def vmem():
    return pl.BlockSpec(memory_space=pltpu.VMEM)


def hbm():
    return pl.BlockSpec(memory_space=pl.ANY)


def dma(*shape):
    return pltpu.SemaphoreType.DMA(shape)


def shape(dims, kind):
    return jax.ShapeDtypeStruct(dims, kind)


def forward(x, gain, bias, w, owt, enc, dect, got):
    return pl.pallas_call(
        forward_kernel,
        out_shape=[
            shape((SEQ, W3), BF),
            shape((3, D, 256), BF),
            shape((NZ, SLAB, SEQ), BF),
            shape((SEQ, 1), F32),
            shape((SEQ, 1), F32),
            shape((SEQ, C), BF),
            shape((256, C), BF),
        ],
        in_specs=[vmem()] * 8,
        out_specs=[vmem(), hbm(), hbm(), vmem(), vmem(), vmem(), vmem()],
        scratch_shapes=[
            pltpu.VMEM((3, D, 256), BF),
            pltpu.VMEM((NZ, SEQ, SLAB), BF),
            pltpu.VMEM((NZ, SLAB, SEQ), BF),
            pltpu.VMEM((SEQ, W3), F32),
            pltpu.VMEM((SEQ, C), BF),
            pltpu.VMEM((256, C), BF),
        ]
        + sum_scratch(SEQ)
        + sum_scratch(256)
        + [dma(2, 4), dma(2, 4), dma(9), dma(9), dma(8), dma(8), pltpu.SemaphoreType.DMA, dma(16)],
        compiler_params=pltpu.CompilerParams(
            collective_id=0, has_side_effects=True, vmem_limit_bytes=56 * 2**20
        ),
    )(x, gain, bias, w, owt, enc, dect, got)


def add_rows(dst, src, count):
    @pl.loop(0, count // 32)
    def _(i):
        here = rows(i * 32, 32)
        dst[here, :] = (dst[here, :].astype(F32) + src[here, :].astype(F32)).astype(BF)


def backward_kernel(
    w_hbm, nt_hbm, qg, qgt, attn, attnt, cg, folded, xhat, gain, go_t, rstd,
    gq, gi_t, code, mixing, gb,
    w, nt, con, xr, rb1, rb, mr,
    cs, cr, ys, yr, xs, xv, ng, lt, gs,
    cp_part, mx_part,
    t_got, t_half, t_ring, t_ss, t_rs,
    d_got, d_half, d_ring, d_ss, d_rs,
    x_ss, x_rs, r1_ss, r1_rs, r_ss, r_rs, m_ss, m_rs,
    cs_ss, cs_rs, y_ss, y_rs, xh_ss, xh_rs, lt_ss, lt_rs, gs_ss, gs_rs, w_sem, nt_sem,
):
    dp, tensor = lax.axis_index("dp"), lax.axis_index("tensor")
    z, xl = dp // 2, rem(dp, 2)
    up, down = rem(z + 1, NZ) * 2 + xl, rem(z + NZ - 1, NZ) * 2 + xl
    other = z * 2 + 1 - xl
    core, q = rem(tensor, 2), tensor // 2
    xh, y = q // NY, rem(q, NY)
    sent = []

    def go(copy):
        copy.start()
        sent.append(copy)

    def order(i):
        odd = rem(i, 2)
        return rem(z + odd * (4 - (i + 1) // 2) + (1 - odd) * (4 + i // 2), NZ)

    def nt_copy(i):
        return pltpu.make_async_copy(nt_hbm.at[order(i)], nt.at[order(i)], nt_sem.at[i])

    for i in range(NZ):
        nt_copy(i).start()
    w_copy = pltpu.make_async_copy(w_hbm, w, w_sem)
    w_copy.start()
    enter()

    base = LR * xl
    crossing, incoming = RB * (1 - xl), RB * xl

    def cross(i):
        return remote(con.at[order(i), rows(crossing, LR), :], xr.at[i], x_ss.at[i], x_rs.at[i], dp=other)

    @pl.loop(0, NZ)
    def _(i):
        nt_copy(i).wait()
        zd = order(i)

        @pl.loop(0, 5)
        def _(k):
            here = rows(k * 128, 128)
            con[zd, here, :] = dot(nt[zd, here, :], qg[...]).astype(BF)

        cross(i).start()

    def add_crossed(i):
        remote(xr.at[i], xr.at[i], x_ss.at[i], x_rs.at[i], dp=other).wait_recv()
        add_rows(con.at[order(i), rows(incoming, LR), :], xr.at[i], LR)

    def chunk(zd, c):
        return con.at[zd, rows(base + c * CH, CH), :]

    ways = ((0, up), (1, down))
    add_crossed(0)
    for way, to in ways:
        go(remote(chunk(order(0), way), rb1.at[way], r1_ss.at[way], r1_rs.at[way], dp=to))

    def ring(s):
        for way, to in ways:
            i = 2 * s - 3 + way
            zd = order(i)
            add_crossed(i)
            for c in (way, 1 - way):
                if s == 2:
                    if c == way:
                        remote(rb1.at[way], rb1.at[way], r1_ss.at[way], r1_rs.at[way], dp=to).wait_recv()
                        add_rows(chunk(zd, c), rb1.at[way], CH)
                else:
                    slot = rb.at[way, s - 3, c]
                    remote(slot, slot, r_ss.at[way, s - 3, c], r_rs.at[way, s - 3, c], dp=to).wait_recv()
                    add_rows(chunk(zd, c), slot, CH)
                go(remote(chunk(zd, c), rb.at[way, s - 2, c], r_ss.at[way, s - 2, c], r_rs.at[way, s - 2, c], dp=to))

    w_copy.wait()

    def feature(i):
        return rem(i, 2) * NY + rem(y + 1 + i // 2, NY)

    def term(block):
        here = rows(block * BLK, BLK)
        out = dot(w[0, here, :], qgt[0:256, :])
        out = out + dot(w[1, here, :], qgt[256:512, :])
        return out + dot(w[2, here, :], qgt[512:768, :])

    def to_core(i):
        return remote(cs.at[i], cr.at[i], cs_ss.at[i], cs_rs.at[i], tensor=q * 2 + 1 - core)

    def to_y(i):
        return remote(
            ys.at[i], yr.at[i], y_ss.at[i], y_rs.at[i], tensor=(xh * NY + rem(y + 1 + i // 2, NY)) * 2 + core
        )

    @pl.loop(0, NQ)
    def _(i):
        cs[i] = term(feature(i) * 2 + 1 - core).astype(BF)
        to_core(i).start()

    def own_block(i):
        total = term(feature(i) * 2 + core)
        to_core(i).wait_recv()
        ys[i] = (total + cr[i].astype(F32)).astype(BF)

    @pl.loop(0, NQ - 2)
    def _(i):
        own_block(i)
        to_y(i).start()

    @pl.loop(NQ - 2, NQ)
    def _(i):
        own_block(i)

    ring(2)
    cp_part[...] = dot(attn[...], folded[...]).astype(BF)
    sum_t = Sum("tensor", cp_part, t_got, t_half, t_ring, code, t_ss, t_rs)
    sum_t.first()
    mx_part[...] = dot(attnt[...], cg[...]).astype(BF)
    sum_d = Sum("dp", mx_part, d_got, d_half, d_ring, mixing, d_ss, d_rs)
    sum_d.first()
    ring(3)

    for i in range(NQ - 2):
        remote(yr.at[i], yr.at[i], y_ss.at[i], y_rs.at[i], tensor=tensor).wait_recv()

    def y_sum(which):
        total = ys[6 + which].astype(F32)
        for k in range(3):
            total = total + yr[2 * k + which].astype(F32)
        return total

    xs[...] = y_sum(1 - xh).astype(BF)
    swap = remote(xs, xv, xh_ss, xh_rs, tensor=((1 - xh) * NY + y) * 2 + core)
    swap.start()
    ng[...] = y_sum(xh)
    sum_t.second()
    sum_d.second()
    swap.wait_recv()

    grad = ng[...] + xv[...].astype(F32)
    ng[...] = grad
    scaled = grad * gain[...]
    hat = xhat[...]
    lt[tensor, 0:1, :] = jnp.sum(scaled, axis=0, keepdims=True)
    lt[tensor, 1:2, :] = jnp.sum(scaled * hat, axis=0, keepdims=True)
    for k in range(1, NR):
        slot = lt.at[tensor]
        go(remote(slot, slot, lt_ss.at[k], lt_rs.at[k], tensor=rem(tensor + k, NR)))

    def fold(v):
        v = v[:, 0:128] + v[:, 128:256] + v[:, 256:384] + v[:, 384:512]
        v = jnp.concatenate([v, jnp.zeros((64, 128), F32)], axis=0)
        return jnp.sum(v.T, axis=0, keepdims=True)

    gs[dp, 0:1, :] = fold(grad * hat)
    gs[dp, 1:2, :] = fold(grad)
    for k in range(1, NR):
        slot = gs.at[dp]
        go(remote(slot, slot, gs_ss.at[k], gs_rs.at[k], dp=rem(dp + k, NR)))

    ring(4)
    sum_t.third()
    sum_d.third()

    for k in range(1, NR):
        slot = lt.at[rem(tensor + NR - k, NR)]
        remote(slot, slot, lt_ss.at[k], lt_rs.at[k], tensor=tensor).wait_recv()
    sums = jnp.sum(lt[...], axis=0)
    lead, trail = sums[0:1, :] * (1.0 / D), sums[1:2, :] * (1.0 / D)
    gi_t[...] = (
        go_t[...].astype(F32) + rstd[...] * (ng[...] * gain[...] - lead - xhat[...] * trail)
    ).astype(BF)
    for k in range(1, NR):
        slot = gs.at[rem(dp + NR - k, NR)]
        remote(slot, slot, gs_ss.at[k], gs_rs.at[k], dp=dp).wait_recv()
    gb[...] = jnp.sum(gs[...], axis=0) * (1.0 / NR)
    sum_t.fourth()
    sum_d.fourth()

    add_crossed(7)
    for c in range(2):
        for way, to in ways:
            slot = rb.at[way, 2, c]
            remote(slot, slot, r_ss.at[way, 2, c], r_rs.at[way, 2, c], dp=to).wait_recv()
            add_rows(chunk(z, c), slot, CH)
    last = remote(con.at[z, rows(BLK - BR * xl, BR), :], mr, m_ss, m_rs, dp=other)
    last.start()
    last.wait_recv()
    add_rows(con.at[z, rows(LR + BR * xl, BR), :], mr, BR)
    for j in range(3):
        gq[j] = con[z, rows(BLK * xl, BLK), j * 256 : (j + 1) * 256].astype(F32) * (1.0 / NR)

    sum_t.last()
    sum_d.last()
    sum_t.drain()
    sum_d.drain()
    last.wait_send()
    swap.wait_send()
    for copy in sent:
        copy.wait_send()

    @pl.loop(0, NZ)
    def _(i):
        cross(i).wait_send()
        to_core(i).wait_send()

    @pl.loop(0, NQ - 2)
    def _(i):
        to_y(i).wait_send()


def backward(*args):
    return pl.pallas_call(
        backward_kernel,
        out_shape=[
            shape((3, BLK, 256), F32),
            shape((BLK, SEQ), BF),
            shape((SEQ, C), BF),
            shape((256, C), BF),
            shape((8, 384), F32),
        ],
        in_specs=[hbm(), hbm()] + [vmem()] * 10,
        out_specs=[vmem()] * 5,
        scratch_shapes=[
            pltpu.VMEM((3, D, 256), BF),
            pltpu.VMEM((NZ, SLAB, SEQ), BF),
            pltpu.VMEM((NZ, SLAB, W3), BF),
            pltpu.VMEM((NZ, LR, W3), BF),
            pltpu.VMEM((2, CH, W3), BF),
            pltpu.VMEM((2, 3, 2, CH, W3), BF),
            pltpu.VMEM((BR, W3), BF),
            pltpu.VMEM((NQ, BLK, SEQ), BF),
            pltpu.VMEM((NQ, BLK, SEQ), BF),
            pltpu.VMEM((NQ, BLK, SEQ), BF),
            pltpu.VMEM((NQ - 2, BLK, SEQ), BF),
            pltpu.VMEM((BLK, SEQ), BF),
            pltpu.VMEM((BLK, SEQ), BF),
            pltpu.VMEM((BLK, SEQ), F32),
            pltpu.VMEM((NR, 8, SEQ), F32),
            pltpu.VMEM((NR, 8, 384), F32),
            pltpu.VMEM((SEQ, C), BF),
            pltpu.VMEM((256, C), BF),
        ]
        + sum_scratch(SEQ)
        + sum_scratch(256)
        + [
            dma(NZ), dma(NZ), dma(2), dma(2), dma(2, 3, 2), dma(2, 3, 2),
            pltpu.SemaphoreType.DMA, pltpu.SemaphoreType.DMA,
            dma(NQ), dma(NQ), dma(NQ), dma(NQ),
            pltpu.SemaphoreType.DMA, pltpu.SemaphoreType.DMA,
            dma(NR), dma(NR), dma(NR), dma(NR), pltpu.SemaphoreType.DMA, dma(NZ),
        ],
        compiler_params=pltpu.CompilerParams(
            collective_id=1, has_side_effects=True, vmem_limit_bytes=60 * 2**20
        ),
    )(*args)


def attention_core(qkv, head_size):
    seq = qkv.shape[0]
    feature_width = qkv.shape[2]
    heads = feature_width // head_size
    split = qkv.reshape(seq, 3, heads, head_size)
    query = split[:, 0]
    keys = split[:, 1]
    values = split[:, 2]
    scores = jnp.einsum("qhd,khd->hqk", query, keys, preferred_element_type=jnp.float32) / jnp.sqrt(
        jnp.float32(head_size)
    )
    row_list = lax.broadcasted_iota(jnp.int32, (seq, seq), 0)
    column_list = lax.broadcasted_iota(jnp.int32, (seq, seq), 1)
    scores = jnp.where((column_list <= row_list)[None], scores, jnp.float32(-1e30))
    top = jnp.max(scores, axis=2, keepdims=True)
    expo = jnp.exp(scores - top)
    probs = expo / jnp.sum(expo, axis=2, keepdims=True)
    mixed = jnp.einsum(
        "hqk,khd->qhd", probs.astype(jnp.bfloat16), values, preferred_element_type=jnp.float32
    )
    return mixed.reshape(seq, feature_width).astype(jnp.bfloat16)


def local(
    residual_in,
    layernorm_gain,
    layernorm_bias,
    qkv_weight,
    out_weight,
    encoder,
    decoder,
    grad_output,
):
    start = lax.axis_index("tensor") * BLK
    qkv, weights, normt, mean, rstd, code_grad, folded = forward(
        residual_in,
        layernorm_gain[None, :],
        layernorm_bias[None, :],
        qkv_weight,
        out_weight.T,
        encoder,
        decoder.T,
        grad_output.T,
    )
    attn, pullback = jax.vjp(lambda t: attention_core(t, HDIM), qkv.reshape(SEQ, 3, 256))
    attn_grad = jnp.dot(code_grad, folded.T, preferred_element_type=F32).astype(BF)
    qkv_grad = pullback(attn_grad)[0].reshape(SEQ, W3)
    columns = lax.dynamic_slice_in_dim(residual_in, start, BLK, 1)
    xhat = ((columns.astype(F32) - mean) * rstd).T
    gain = lax.dynamic_slice_in_dim(layernorm_gain, start, BLK, 0)
    grad_qkv, grad_input, code, mixing, sums = backward(
        weights, normt, qkv_grad, qkv_grad.T, attn, attn.T, code_grad, folded,
        xhat, gain[:, None], grad_output.T, rstd.reshape(1, SEQ),
    )
    residual_out = (columns.astype(F32) + jnp.dot(code, decoder, preferred_element_type=F32)).astype(BF)
    grad_out_weight = lax.dot_general(
        mixing, encoder, (((1,), (1,)), ((), ())), preferred_element_type=F32
    ) * (1.0 / NR)
    return residual_out, grad_input.T, grad_qkv, grad_out_weight, sums[0, :BLK], sums[1, :BLK]


def solution(mesh):
    in_specs = (
        P("dp", None),
        P(),
        P(),
        P(None, "dp", "tensor"),
        P("tensor", "dp"),
        P("dp", None),
        P(None, "tensor"),
        P("dp", "tensor"),
    )
    out_specs = (
        P("dp", "tensor"),
        P("dp", "tensor"),
        P(None, "dp", "tensor"),
        P("tensor", "dp"),
        P("tensor"),
        P("tensor"),
    )
    return jax.shard_map(local, mesh=mesh, in_specs=in_specs, out_specs=out_specs, check_vma=False)
```

time: 901 us -> 222 us (0.25)
  waiting for transfers between devices: 715 us -> 0 us
  Pallas kernels: 0 us -> 195 us
  blocking collectives: 80.7 us -> 0 us
  matrix products: 48.5 us -> 9.39 us
  other arithmetic: 31.3 us -> 2.82 us
  between operations: 14.3 us -> 0.86 us
    psum x3 -> x0, waiting for transfers between devices: 361 us -> none  [the longest x1 155 us: local(): code = lax.psum(code_part.astype(jnp.bfloat16), 'tensor')]
    pallas_call x0 -> x2, Pallas kernels: none -> 195 us  [the longest x1 107 us: backward(): pl.pallas_call(backward_kernel, out_shape=[shape((3, BLK, 256), F32), sha...]
    reduce_scatter x2 -> x0, waiting for transfers between devices: 193 us -> none  [the longest x1 103 us: local(): lax.psum_scatter(input_part.astype(jnp.bfloat16), 'tensor', scatter_dimen...]
    all_gather x1 -> x0, waiting for transfers between devices: 160 us -> none  [local(): weights = lax.all_gather(qkv_weight, 'dp', axis=1, tiled=True)]
    psum x2 -> x0, blocking collectives: 80.7 us -> none  [the longest x1 52.1 us: local(): lax.psum((jnp.sum(scaled_rows, axis=1), jnp.sum(scaled_rows * centered_co...]
    dot_general x10 -> x3, matrix products: 42.5 us -> 4.78 us  [the longest x1 2.36 us: local(): jnp.dot(code, decoder, preferred_element_type=F32)]
    convert_element_type x2 -> x0, other arithmetic: 10 us -> none  [the longest x1 7.84 us: local(): input_float = residual_in.astype(jnp.float32)]
  transfers between devices with their start and end apart: 6 -> 0, of which waited for: 6 -> 0; matrix products, arithmetic and copies ran while one was open for 8% -> 0% of each run, Pallas kernels for 0% -> 0%
where the time goes in v1:
time: 222 us; the launch traced here: 219 us
  Pallas kernels  195 us (88%)
  local copies, waits for them, and re-layouts  11 us (5%)
  matrix products  9.39 us (4%)
  other arithmetic  2.82 us (1%)
    pallas_call x1, Pallas kernels, backward(): pl.pallas_call(backward_kernel, out_shape=[shape((3, BLK, 256), F32), sha...  107 us
    pallas_call x1, Pallas kernels, forward(): pl.pallas_call(forward_kernel, out_shape=[shape((SEQ, W3), BF), shape((3,...  87.2 us

profile of v1, /device:TPU:1, one launch (start us, length us, event | category | flops | bytes accessed | tf_op | source)
XLA Modules:
  0.0 218.8 jit_solution(14588398188220494902)
XLA Ops:
  0.6 87.2 %shard_map.127 = (bf16[512,768]{1,0:T(8,128)(2,1)}, bf16[3,5120,256]{2,1,0:T(8,128)(2,1)}, bf16[8,640,512]{2,1,0:T(8,128)(2,1)}, f32[512,1]{1,0:T(8,128)}, f32[5...) custom-call(bf16[512,5120]{1,0:T(8,128)(2,1)} %x.7, f32[1,5120]{1,0:T(1,128)} %bitcast.71, ...), custom_call_target="tpu_custom_call" | custom-call | tf_op jit(solution)/shard_map/pallas_call | solution.py:299
  87.9 2.2 %reshape_reshape.3 = bf16[512,3,2,128]{3,2,1,0:T(2,128)(2,1)S(1)} reshape(bf16[512,768]{1,0:T(8,128)(2,1)} %get-tuple-element.22) | data formatting | bytes 1572864 | tf_op jit(solution)/shard_map/jvp()/reshape;reshape | solution.py:605
  90.1 0.5 fusion.30
  90.8 0.6 fusion.31
  91.3 0.3 fusion.4
  91.9 0.4 convolution_convert_fusion.3
  92.3 0.6 fusion.3
  93.0 1.1 divide_convert_fusion
  94.1 1.3 fusion.11
  95.4 1.3 fusion.12
  96.7 0.5 fusion.10
  97.2 1.2 copy.38.qg
  98.4 0.3 convolution_convert_fusion.1
  98.8 0.8 copy.39.attn
  99.6 1.2 constant_dynamic-slice_fusion
  101.4 1.0 fusion.22.xhat
  102.3 0.8 dynamic_slice.7
  103.1 0.8 broadcast_in_dim.57.gain
  103.9 107.4 %shard_map.128 = (f32[3,320,256]{2,1,0:T(8,128)}, bf16[320,512]{1,0:T(8,128)(2,1)}, bf16[512,640]{1,0:T(8,128)(2,1)}, bf16[256,640]{1,0:T(8,128)(2,1)}, f32[8,384]{1,0:T(8,128)}) custom-call(bf16[3,5120,256]{2,1,0:T(8,128)(2,1)} %get-tuple-element.18.w_hbm, bf16[8,640,512]{2,1,0:T(8,128)(2,1)} %get-tuple-element.19.nt_hbm, bf16[512,768]{1,0:T(8,128)(2,1)} %copy.38.qg, ...), custom_call_target="tpu_custom_call" | custom-call | tf_op jit(solution)/shard_map/pallas_call | solution.py:555
  211.3 2.4 %fusion.7 = bf16[512,320]{0,1:T(8,128)(2,1)} fusion(bf16[512,640]{1,0:T(8,128)(2,1)} %get-tuple-element.25, bf16[640,320]{0,1:T(8,128)(2,1)S(1)} %copy-done.4, bf16[512,320]{0,1:T(8,128)(2,1)S(1)} %copy.48), kind=kOutput, calls=%fused_computation.16 | convolution fusion | flops 210206720 | bytes 1720320 | tf_op jit(solution)/shard_map/dot_general | solution.py:655
  213.7 2.0 convolution_multiply_fusion
  215.7 1.4 slice_reduce_fusion
  217.1 0.7 copy.72
  217.8 0.9 copy.73
  (30 shorter events, 0.9 us)
Async XLA Ops:
  90.7 1.1 copy-start.1
  90.7 1.2 copy-start.5
  97.2 3.6 %copy-start = (bf16[512,3,2,128]{0,3,2,1:T(8,128)(2,1)}, bf16[512,3,2,128]{0,3,2,1:T(8,128)(2,1)S(1)}, u32[]{:S(2)}) copy-start(bf16[512,3,2,128]{0,3,2,1:T(8,128)(2,1)S(1)} %pad_add_fusion) | copy-start | bytes 2359300
  98.4 2.6 %copy-start.9 = (f32[512,1]{1,0:T(8,128)S(1)}, f32[512,1]{1,0:T(8,128)}, u32[]{:S(2)}) copy-start(f32[512,1]{1,0:T(8,128)} %get-tuple-element.24) | copy-start | bytes 6148
  98.4 2.8 %copy-start.8 = (f32[512,1]{1,0:T(8,128)S(1)}, f32[512,1]{1,0:T(8,128)}, u32[]{:S(2)}) copy-start(f32[512,1]{1,0:T(8,128)} %get-tuple-element.23) | copy-start | bytes 6148
  98.7 5.1 %copy-start.2 = (bf16[2,128,512]{2,1,0:T(8,128)(2,1)}, bf16[2,128,512]{2,1,0:T(8,128)(2,1)S(1)}, u32[]{:S(2)}) copy-start(bf16[2,128,512]{2,1,0:T(8,128)(2,1)S(1)} %convolution_convert_fusion.1) | copy-start | bytes 786436
  101.2 2.7 %copy-start.10 = (f32[512]{0:T(512)}, f32[512]{0:T(512)S(1)}, u32[]{:S(2)}) copy-start(f32[512]{0:T(512)S(1)} %reduce.1) | copy-start | bytes 6148
  103.9 107.5 %copy-start.4 = (bf16[640,320]{0,1:T(8,128)(2,1)S(1)}, bf16[640,320]{0,1:T(8,128)(2,1)}, u32[]{:S(2)}) copy-start(bf16[640,320]{0,1:T(8,128)(2,1)} %param.14) | copy-start | bytes 1228804
  103.9 109.8 %copy-start.3 = (bf16[320,640]{1,0:T(8,128)(2,1)S(1)}, bf16[320,640]{1,0:T(8,128)(2,1)}, u32[]{:S(2)}) copy-start(bf16[320,640]{1,0:T(8,128)(2,1)} %enc.1) | copy-start | bytes 1228804
  211.3 5.8 %copy-start.7 = (bf16[320,512]{1,0:T(8,128)(2,1)S(1)}, bf16[320,512]{1,0:T(8,128)(2,1)}, u32[]{:S(2)}) copy-start(bf16[320,512]{1,0:T(8,128)(2,1)} %get-tuple-element.26) | copy-start | bytes 983044
  211.3 6.5 %copy-start.6 = (f32[3,320,256]{2,1,0:T(8,128)S(1)}, f32[3,320,256]{2,1,0:T(8,128)}, u32[]{:S(2)}) copy-start(f32[3,320,256]{2,1,0:T(8,128)} %get-tuple-element.53) | copy-start | bytes 2949124

commit v2 on v1

v2 whole, which is shorter than its diff:
```python
import functools

import jax
import jax.numpy as jnp
from jax import lax
from jax.experimental import pallas as pl
from jax.experimental.pallas import tpu as pltpu
from jax.sharding import PartitionSpec as P

HDIM = 128
EPS = 1e-05
MESH = pl.DeviceIdType.MESH
F32, BF = jnp.float32, jnp.bfloat16

NZ, NY, NQ, NR = 8, 4, 8, 16
SEQ, D, C, W3 = 512, 5120, 640, 768
BLK = 320
SLAB = 640
LR = 160
RB = SLAB - LR
CH = RB // 2
BR = BLK - LR


def rem(a, n):
    return lax.rem(a, n)


def rows(start, size):
    return pl.ds(pl.multiple_of(start, 16), size)


def dot(a, b):
    return lax.dot_general(a, b, (((1,), (0,)), ((), ())), preferred_element_type=F32)


def dot_nt(a, b):
    return lax.dot_general(a, b, (((1,), (1,)), ((), ())), preferred_element_type=F32)


def dot_tn(a, b):
    return lax.dot_general(a, b, (((0,), (0,)), ((), ())), preferred_element_type=F32)


def remote(src, dst, ssem, rsem, **device):
    return pltpu.make_async_remote_copy(
        src_ref=src, dst_ref=dst, send_sem=ssem, recv_sem=rsem, device_id=device, device_id_type=MESH
    )


def enter():
    barrier = pltpu.get_barrier_semaphore()
    for axis in ("dp", "tensor"):
        me = lax.axis_index(axis)
        for k in range(1, NR):
            pl.semaphore_signal(barrier, inc=1, device_id={axis: rem(me + k, NR)}, device_id_type=MESH)
    pl.semaphore_wait(barrier, 2 * (NR - 1))


class Sum:
    def __init__(self, axis, part, out, buffers):
        self.axis, self.part, self.out = axis, part, out
        self.got, self.half, self.ring, self.mid, self.mid_got, self.ssem, self.rsem = buffers
        index = lax.axis_index(axis)
        self.n = self.ring.shape[0]
        self.a = rem(index, 2)
        self.q = rem(index // 2, self.n)
        self.top = index // (2 * self.n)
        self.h = part.shape[0] // 2
        self.b = self.h // self.n
        self.sent = []

    def at(self, top, q, a):
        return {self.axis: (top * self.n + q) * 2 + a}

    def pair(self):
        return self.at(self.top, self.q, 1 - self.a)

    def peer(self, k):
        return self.at(self.top, rem(self.q + k, self.n), self.a)

    def over(self):
        return self.at(1 - self.top, self.q, self.a)

    def go(self, copy):
        copy.start()
        self.sent.append(copy)

    def first(self):
        src = self.part.at[rows((1 - self.a) * self.h, self.h), :]
        self.go(remote(src, self.got, self.ssem.at[0], self.rsem.at[0], **self.pair()))

    def second(self):
        remote(self.got, self.got, self.ssem.at[0], self.rsem.at[0], **self.pair()).wait_recv()
        mine = self.part[rows(self.a * self.h, self.h), :].astype(F32)
        self.half[...] = (mine + self.got[...].astype(F32)).astype(BF)
        for k in range(1, self.n):
            to = rem(self.q + k, self.n)
            src = self.half.at[rows(to * self.b, self.b), :]
            self.go(remote(src, self.ring.at[self.q], self.ssem.at[k], self.rsem.at[k], **self.peer(k)))

    def reduced(self):
        total = self.half[rows(self.q * self.b, self.b), :].astype(F32)
        for k in range(1, self.n):
            source = rem(self.q + self.n - k, self.n)
            slot = self.ring.at[source]
            remote(slot, slot, self.ssem.at[k], self.rsem.at[k], **self.peer(k)).wait_recv()
            total = total + self.ring[source].astype(F32)
        return total

    def spread(self, total):
        here = rows(self.a * self.h + self.q * self.b, self.b)
        self.out[here, :] = total.astype(BF)
        piece = self.out.at[here, :]
        for k in range(1, self.n):
            self.go(remote(piece, piece, self.ssem.at[7 + k], self.rsem.at[7 + k], **self.peer(k)))

    def third(self):
        if self.mid is None:
            self.spread(self.reduced())
        else:
            self.mid[...] = self.reduced().astype(BF)
            self.go(remote(self.mid, self.mid_got, self.ssem.at[16], self.rsem.at[16], **self.over()))

    def across(self):
        remote(self.mid, self.mid_got, self.ssem.at[16], self.rsem.at[16], **self.over()).wait_recv()
        self.spread(self.mid[...].astype(F32) + self.mid_got[...].astype(F32))

    def fourth(self):
        for k in range(1, self.n):
            source = rem(self.q + self.n - k, self.n)
            piece = self.out.at[rows(self.a * self.h + source * self.b, self.b), :]
            remote(piece, piece, self.ssem.at[7 + k], self.rsem.at[7 + k], **self.peer(k)).wait_recv()
        mine = self.out.at[rows(self.a * self.h, self.h), :]
        self.go(remote(mine, mine, self.ssem.at[15], self.rsem.at[15], **self.pair()))

    def last(self):
        other = self.out.at[rows((1 - self.a) * self.h, self.h), :]
        remote(other, other, self.ssem.at[15], self.rsem.at[15], **self.pair()).wait_recv()

    def drain(self):
        for copy in self.sent:
            copy.wait_send()


def dma(*shape):
    return pltpu.SemaphoreType.DMA(shape)


def sum_buffers(r, n):
    h = r // 2
    cut = pltpu.VMEM((h // n, C), BF)
    mids = [cut, cut] if n == NY else [None, None]
    return [pltpu.VMEM((h, C), BF), pltpu.VMEM((h, C), BF), pltpu.VMEM((n, h // n, C), BF)] + mids + [dma(17), dma(17)]


def add_rows(dst, src, count):
    @pl.loop(0, count // 80)
    def _(i):
        here = rows(i * 80, 80)
        dst[here, :] = (dst[here, :].astype(F32) + src[here, :].astype(F32)).astype(BF)


def kernel(
    x_hbm, gain, bias, w_in, owt, enc, dect, got,
    ro_t, gi_t, gq, gow_t, gb,
    x, w, nt, acc, mu, rstd, xt, gcol, hat, st,
    cg_part, fo_part, cg, folded, qkv, ag, attn, qg, qgt, dkv,
    con, xr, rb1, rb, mr, cs, cr, ys, yr, xs, xv, ng, lt, gs, cp_part, mx_part, code, mixing,
    t1, d1, t2, d2,
    x_sem, loc, a_ss, a_rs, b_ss, b_rs, c_ss, c_rs,
    x_ss, x_rs, r1_ss, r1_rs, r_ss, r_rs, m_ss, m_rs,
    cs_ss, cs_rs, y_ss, y_rs, xh_ss, xh_rs, lt_ss, lt_rs, gs_ss, gs_rs,
):
    dp, tensor = lax.axis_index("dp"), lax.axis_index("tensor")
    z, xl = dp // 2, rem(dp, 2)
    up, down = rem(z + 1, NZ) * 2 + xl, rem(z + NZ - 1, NZ) * 2 + xl
    other = z * 2 + 1 - xl
    core, q = rem(tensor, 2), tensor // 2
    xh, y = q // NY, rem(q, NY)
    ways = ((0, up), (1, down))
    sent = []

    def go(copy):
        copy.start()
        sent.append(copy)

    x_copies = [
        pltpu.make_async_copy(x_hbm.at[pl.ds(i * 256, 256), :], x.at[pl.ds(i * 256, 256), :], x_sem.at[i])
        for i in range(2)
    ]
    for copy in x_copies:
        copy.start()

    def block(zs, offset, size):
        return w.at[:, rows(zs * SLAB + offset, size), :]

    own = BLK * xl
    shared = BLK - BR * xl
    crossing = RB * xl
    incoming = RB * (1 - xl)

    enter()
    mine = pltpu.make_async_copy(w_in, block(z, own, BLK), loc)
    mine.start()
    first = LR * (1 - xl)
    go(remote(w_in.at[:, rows(first, BR), :], block(z, own + first, BR), b_ss.at[0], b_rs.at[0], dp=other))
    for way, to in ways:
        go(remote(w_in, block(z, own, BLK), a_ss.at[way, 0], a_rs.at[way, 0], dp=to))
    go(remote(w_in.at[:, rows(BR * xl, LR), :], block(z, crossing, LR), c_ss.at[0], c_rs.at[0], dp=other))

    def slab_cols(zs):
        return pl.ds(pl.multiple_of(zs * SLAB, 128), SLAB)

    def norm(lo, hi):
        @pl.loop(lo, hi)
        def _(i):
            here = rows(i * 16, 16)
            v = x[here, :].astype(F32)
            mean = jnp.sum(v, axis=1, keepdims=True) * (1.0 / D)
            v = v - mean
            var = jnp.sum(v * v, axis=1, keepdims=True) * (1.0 / D)
            scale = lax.rsqrt(var + EPS)
            mu[here, :] = jnp.broadcast_to(mean, (16, 128))
            rstd[here, :] = jnp.broadcast_to(scale, (16, 128))
            x[here, :] = (v * scale * gain[...] + bias[...]).astype(BF)

    for copy in x_copies:
        copy.wait()

    @pl.loop(0, 4)
    def _(i):
        here = pl.ds(pl.multiple_of(i * 128, 128), 128)
        xt[:, here] = x[here, slab_cols(q)].T

    norm(0, 14)
    piece = block(z, shared, BR)
    remote(piece, piece, b_ss.at[0], b_rs.at[0], dp=other).wait_recv()
    for way, to in ways:
        go(remote(piece, piece, b_ss.at[1 + way * 4], b_rs.at[1 + way * 4], dp=to))
    norm(14, 32)

    def slabs(s):
        return ((0, up, rem(z + NZ - s, NZ)), (1, down, rem(z + s, NZ)))

    def step_a(s):
        for way, to, zs in slabs(s):
            part = block(zs, own, BLK)
            remote(part, part, a_ss.at[way, s - 1], a_rs.at[way, s - 1], dp=to).wait_recv()
            if s == 3:
                part = block(zs, own + way * (BLK // 2), BLK // 2)
            go(remote(part, part, a_ss.at[way, s], a_rs.at[way, s], dp=to))
            part = block(zs, crossing, LR)
            k = s + way * 3
            go(remote(part, part, c_ss.at[k], c_rs.at[k], dp=other))

    def step_b(s):
        for way, to, zs in slabs(s):
            part = block(zs, shared, BR)
            k = s + way * 4
            remote(part, part, b_ss.at[k], b_rs.at[k], dp=to).wait_recv()
            if s == 3:
                part = block(zs, shared + way * (BR // 2), BR // 2)
            go(remote(part, part, b_ss.at[k + 1], b_rs.at[k + 1], dp=to))

    def use(zs, k, begin=False):
        part = block(zs, incoming, LR)
        remote(part, part, c_ss.at[k], c_rs.at[k], dp=other).wait_recv()

        @pl.loop(0, 2)
        def _(i):
            here = rows(i * 256, 256)
            a = x[here, slab_cols(zs)]
            for j in range(3):
                cols = slice(j * 256, (j + 1) * 256)
                term = dot(a, w[j, rows(zs * SLAB, SLAB), :])
                if begin:
                    acc[here, cols] = term
                else:
                    acc[here, cols] += term

    def turn(zs):
        @pl.loop(0, 4)
        def _(i):
            here = pl.ds(pl.multiple_of(i * 128, 128), 128)
            nt[zs, :, here] = x[here, slab_cols(zs)].T

    step_a(1)
    cg_part[...] = dot_tn(got[...], dect[...]).astype(BF)
    sum_t = Sum("tensor", cg_part, cg, t1)
    sum_t.first()
    fo_part[...] = dot_tn(owt[...], enc[...]).astype(BF)
    sum_d = Sum("dp", fo_part, folded, d1)
    sum_d.first()
    step_b(1)
    mine.wait()
    use(z, 0, True)
    sum_t.second()
    turn(z)
    turn(rem(z + 4, NZ))
    step_a(2)
    sum_d.second()
    sum_t.third()
    use(rem(z + NZ - 1, NZ), 1)
    use(rem(z + 1, NZ), 4)
    step_b(2)
    sum_t.across()
    for k in (1, 2, 3):
        turn(rem(z + NZ - k, NZ))
        turn(rem(z + k, NZ))
    mu_row = mu[...].T[0:1, :]
    rs_row = rstd[...].T[0:1, :]
    gcol[...] = jnp.broadcast_to(gain[0:1, slab_cols(q)], (128, SLAB)).T
    mine_rows = rows(core * BLK, BLK)
    hat[...] = (xt[mine_rows, :].astype(F32) - mu_row) * rs_row
    st[0:1, :] = rs_row
    step_a(3)
    sum_d.third()
    sum_t.fourth()
    use(rem(z + NZ - 2, NZ), 2)
    use(rem(z + 2, NZ), 5)
    step_b(3)
    sum_d.fourth()
    sum_t.last()
    z4 = rem(z + 4, NZ)
    for way, to in ways:
        part = block(z4, own + way * (BLK // 2), BLK // 2)
        remote(part, part, a_ss.at[way, 3], a_rs.at[way, 3], dp=to).wait_recv()
    part = block(z4, crossing, LR)
    go(remote(part, part, c_ss.at[7], c_rs.at[7], dp=other))
    use(rem(z + NZ - 3, NZ), 3)
    use(rem(z + 3, NZ), 6)
    sum_d.last()
    ag[...] = dot_nt(cg[...], folded[...]).astype(BF)
    for way, to in ways:
        part = block(z4, shared + way * (BR // 2), BR // 2)
        remote(part, part, b_ss.at[4 + way * 4], b_rs.at[4 + way * 4], dp=to).wait_recv()
    use(z4, 7)
    qkv[...] = acc[...].astype(BF)

    dkv[...] = jnp.zeros_like(dkv)
    rate = HDIM**-0.5
    for h in range(2):
        cq = slice(h * HDIM, (h + 1) * HDIM)
        ck = slice(256 + h * HDIM, 256 + (h + 1) * HDIM)
        cv = slice(512 + h * HDIM, 512 + (h + 1) * HDIM)
        for r in range(4):
            here, n = slice(r * 128, (r + 1) * 128), 128 * (r + 1)
            qb, kb, vb = qkv[here, cq], qkv[0:n, ck], qkv[0:n, cv]
            s = dot_nt(qb, kb) * rate
            at_row = lax.broadcasted_iota(jnp.int32, (128, n), 0) + r * 128
            at_col = lax.broadcasted_iota(jnp.int32, (128, n), 1)
            s = jnp.where(at_col <= at_row, s, -1e30)
            e = jnp.exp(s - jnp.max(s, axis=1, keepdims=True))
            p = e * (1.0 / jnp.sum(e, axis=1, keepdims=True))
            pb = p.astype(BF)
            attn[here, cq] = dot(pb, vb).astype(BF)
            da = ag[here, cq]
            dpr = dot_nt(da, vb).astype(BF).astype(F32)
            ds = p * (dpr - jnp.sum(p * dpr, axis=1, keepdims=True))
            ds = (ds * rate).astype(BF)
            qg[here, cq] = dot(ds, kb).astype(BF)
            dkv[0:n, cq] += dot_tn(ds, qb)
            dkv[0:n, ck] += dot_tn(pb, da)
    qg[:, 256:768] = dkv[...].astype(BF)

    def order(i):
        odd = rem(i, 2)
        return rem(z + odd * (4 - (i + 1) // 2) + (1 - odd) * (4 + i // 2), NZ)

    base = LR * xl
    leaving, arriving = RB * (1 - xl), RB * xl

    def cross(i):
        return remote(con.at[order(i), rows(leaving, LR), :], xr.at[i], x_ss.at[i], x_rs.at[i], dp=other)

    def contribute(lo, hi):
        @pl.loop(lo, hi)
        def _(i):
            zd = order(i)

            @pl.loop(0, 5)
            def _(k):
                here = rows(k * 128, 128)
                con[zd, here, :] = dot(nt[zd, here, :], qg[...]).astype(BF)

            cross(i).start()

    def add_crossed(i):
        remote(xr.at[i], xr.at[i], x_ss.at[i], x_rs.at[i], dp=other).wait_recv()
        add_rows(con.at[order(i), rows(arriving, LR), :], xr.at[i], LR)

    def chunk(zd, n):
        c = (1 - xl) * (1 - n) + xl * n
        return con.at[zd, rows(base + c * CH, CH), :]

    def begin(way, to):
        go(remote(chunk(order(0), way), rb1.at[way], r1_ss.at[way], r1_rs.at[way], dp=to))

    def ring(s, n):
        for way, to in ways:
            i = 2 * s - 3 + way
            zd = order(i)
            if n == 1:
                add_crossed(i)
            if s == 2:
                if n == way:
                    remote(rb1.at[way], rb1.at[way], r1_ss.at[way], r1_rs.at[way], dp=to).wait_recv()
                    add_rows(chunk(zd, n), rb1.at[way], CH)
            else:
                slot = rb.at[way, s - 3, n]
                remote(slot, slot, r_ss.at[way, s - 3, n], r_rs.at[way, s - 3, n], dp=to).wait_recv()
                add_rows(chunk(zd, n), slot, CH)
            go(remote(chunk(zd, n), rb.at[way, s - 2, n], r_ss.at[way, s - 2, n], r_rs.at[way, s - 2, n], dp=to))

    def feature(i):
        return rem(i, 2) * NY + rem(y + 1 + i // 2, NY)

    def term(index):
        here = rows(index * BLK, BLK)
        out = dot(w[0, here, :], qgt[0:256, :])
        out = out + dot(w[1, here, :], qgt[256:512, :])
        return out + dot(w[2, here, :], qgt[512:768, :])

    def to_core(i):
        return remote(cs.at[i], cr.at[i], cs_ss.at[i], cs_rs.at[i], tensor=q * 2 + 1 - core)

    def to_y(i):
        there = (xh * NY + rem(y + 1 + i // 2, NY)) * 2 + core
        return remote(ys.at[i], yr.at[i], y_ss.at[i], y_rs.at[i], tensor=there)

    def other_blocks(lo, hi):
        @pl.loop(lo, hi)
        def _(i):
            cs[i] = term(feature(i) * 2 + 1 - core).astype(BF)
            to_core(i).start()

    def own_block(i):
        total = term(feature(i) * 2 + core)
        to_core(i).wait_recv()
        ys[i] = (total + cr[i].astype(F32)).astype(BF)

    contribute(0, 1)
    begin(0, up)
    contribute(1, 4)

    @pl.loop(0, 6)
    def _(i):
        here = pl.ds(pl.multiple_of(i * 128, 128), 128)
        qgt[here, :] = qg[:, here].T

    add_crossed(0)
    begin(1, down)
    contribute(4, NZ)
    other_blocks(0, NQ)
    ring(2, 0)
    ring(2, 1)

    @pl.loop(0, NQ - 2)
    def _(i):
        own_block(i)
        to_y(i).start()

    @pl.loop(NQ - 2, NQ)
    def _(i):
        own_block(i)

    ring(3, 0)
    cp_part[...] = dot(attn[...], folded[...]).astype(BF)
    sum_t2 = Sum("tensor", cp_part, code, t2)
    sum_t2.first()
    mx_part[...] = dot_tn(attn[...], cg[...]).astype(BF)
    sum_d2 = Sum("dp", mx_part, mixing, d2)
    sum_d2.first()
    ring(3, 1)
    sum_t2.second()
    sum_d2.second()
    ring(4, 0)
    sum_t2.third()

    for i in range(NQ - 2):
        remote(yr.at[i], yr.at[i], y_ss.at[i], y_rs.at[i], tensor=tensor).wait_recv()

    def y_sum(which):
        total = ys[6 + which].astype(F32)
        for k in range(3):
            total = total + yr[2 * k + which].astype(F32)
        return total

    xs[...] = y_sum(1 - xh).astype(BF)
    swap = remote(xs, xv, xh_ss, xh_rs, tensor=((1 - xh) * NY + y) * 2 + core)
    swap.start()
    ng[...] = y_sum(xh)
    sum_d2.third()
    ring(4, 1)
    sum_t2.across()
    swap.wait_recv()

    grad = ng[...] + xv[...].astype(F32)
    ng[...] = grad
    scaled = grad * gcol[mine_rows, 0:1]
    lt[tensor, 0:1, :] = jnp.sum(scaled, axis=0, keepdims=True)
    lt[tensor, 1:2, :] = jnp.sum(scaled * hat[...], axis=0, keepdims=True)
    slot = lt.at[tensor]
    for k in range(1, NR):
        go(remote(slot, slot, lt_ss.at[k], lt_rs.at[k], tensor=rem(tensor + k, NR)))

    def fold(v):
        v = v[:, 0:128] + v[:, 128:256] + v[:, 256:384] + v[:, 384:512]
        v = jnp.concatenate([v, jnp.zeros((64, 128), F32)], axis=0)
        return jnp.sum(v.T, axis=0, keepdims=True)

    gs[dp, 0:1, :] = fold(ng[...] * hat[...])
    gs[dp, 1:2, :] = fold(ng[...])
    slot = gs.at[dp]
    for k in range(1, NR):
        go(remote(slot, slot, gs_ss.at[k], gs_rs.at[k], dp=rem(dp + k, NR)))
    sum_d2.fourth()
    sum_t2.fourth()

    for k in range(1, NR):
        slot = lt.at[rem(tensor + NR - k, NR)]
        remote(slot, slot, lt_ss.at[k], lt_rs.at[k], tensor=tensor).wait_recv()
    sums = jnp.sum(lt[...], axis=0)
    lead, trail = sums[0:1, :] * (1.0 / D), sums[1:2, :] * (1.0 / D)
    scaled = ng[...] * gcol[mine_rows, 0:1]
    gi_t[...] = (got[...].astype(F32) + st[0:1, :] * (scaled - lead - hat[...] * trail)).astype(BF)

    def close(n):
        for way, to in ways:
            slot = rb.at[way, 2, n]
            remote(slot, slot, r_ss.at[way, 2, n], r_rs.at[way, 2, n], dp=to).wait_recv()
            add_rows(chunk(z, n), slot, CH)

    close(0)
    last = remote(con.at[z, rows(BLK - BR * xl, BR), :], mr, m_ss, m_rs, dp=other)
    last.start()
    sum_t2.last()
    ro_t[...] = (xt[mine_rows, :].astype(F32) + dot_nt(dect[...], code[...])).astype(BF)
    sum_d2.last()
    gow_t[...] = dot_nt(enc[...], mixing[...]) * (1.0 / NR)
    for k in range(1, NR):
        slot = gs.at[rem(dp + NR - k, NR)]
        remote(slot, slot, gs_ss.at[k], gs_rs.at[k], dp=dp).wait_recv()
    gb[...] = jnp.sum(gs[...], axis=0) * (1.0 / NR)
    add_crossed(7)
    close(1)
    last.wait_recv()
    add_rows(con.at[z, rows(LR + BR * xl, BR), :], mr, BR)
    for j in range(3):
        gq[j] = con[z, rows(BLK * xl, BLK), j * 256 : (j + 1) * 256].astype(F32) * (1.0 / NR)

    for total in (sum_t, sum_d, sum_t2, sum_d2):
        total.drain()
    last.wait_send()
    swap.wait_send()
    for copy in sent:
        copy.wait_send()

    @pl.loop(0, NZ)
    def _(i):
        cross(i).wait_send()
        to_core(i).wait_send()

    @pl.loop(0, NQ - 2)
    def _(i):
        to_y(i).wait_send()


def sublayer(*args):
    def shape(dims, kind):
        return jax.ShapeDtypeStruct(dims, kind)

    def v(kind, *dims):
        return pltpu.VMEM(dims, kind)

    one = pltpu.SemaphoreType.DMA
    whole = pl.BlockSpec(memory_space=pltpu.VMEM)
    far = pl.BlockSpec(memory_space=pl.ANY)
    scratch = [
        v(BF, SEQ, D), v(BF, 3, D, 256), v(BF, NZ, SLAB, SEQ), v(F32, SEQ, W3), v(F32, SEQ, 128), v(F32, SEQ, 128),
        v(BF, SLAB, SEQ), v(F32, SLAB, 128), v(F32, BLK, SEQ), v(F32, 8, SEQ),
        v(BF, SEQ, C), v(BF, 256, C), v(BF, SEQ, C), v(BF, 256, C), v(BF, SEQ, W3), v(BF, SEQ, 256),
        v(BF, SEQ, 256), v(BF, SEQ, W3), v(BF, W3, SEQ), v(F32, SEQ, 512),
        v(BF, NZ, SLAB, W3), v(BF, NZ, LR, W3), v(BF, 2, CH, W3), v(BF, 2, 3, 2, CH, W3), v(BF, BR, W3),
        v(BF, NQ, BLK, SEQ), v(BF, NQ, BLK, SEQ), v(BF, NQ, BLK, SEQ), v(BF, NQ - 2, BLK, SEQ),
        v(BF, BLK, SEQ), v(BF, BLK, SEQ), v(F32, BLK, SEQ), v(F32, NR, 8, SEQ), v(F32, NR, 8, 384),
        v(BF, SEQ, C), v(BF, 256, C), v(BF, SEQ, C), v(BF, 256, C),
        sum_buffers(SEQ, NY), sum_buffers(256, NZ), sum_buffers(SEQ, NY), sum_buffers(256, NZ),
        dma(2), one, dma(2, 4), dma(2, 4), dma(9), dma(9), dma(8), dma(8),
        dma(NZ), dma(NZ), dma(2), dma(2), dma(2, 3, 2), dma(2, 3, 2), one, one,
        dma(NQ), dma(NQ), dma(NQ), dma(NQ), one, one, dma(NR), dma(NR), dma(NR), dma(NR),
    ]
    return pl.pallas_call(
        kernel,
        out_shape=[
            shape((BLK, SEQ), BF),
            shape((BLK, SEQ), BF),
            shape((3, BLK, 256), F32),
            shape((BLK, 256), F32),
            shape((8, 384), F32),
        ],
        in_specs=[far, whole, whole, far, whole, whole, whole, whole],
        out_specs=[whole] * 5,
        scratch_shapes=scratch,
        compiler_params=pltpu.CompilerParams(
            collective_id=0, has_side_effects=True, vmem_limit_bytes=62 * 2**20
        ),
    )(*args)


def local(
    residual_in,
    layernorm_gain,
    layernorm_bias,
    qkv_weight,
    out_weight,
    encoder,
    decoder,
    grad_output,
):
    residual_out, grad_input, grad_qkv, grad_out_weight, sums = sublayer(
        residual_in,
        layernorm_gain[None, :],
        layernorm_bias[None, :],
        qkv_weight,
        out_weight.T,
        encoder,
        decoder.T,
        grad_output.T,
    )
    return residual_out.T, grad_input.T, grad_qkv, grad_out_weight.T, sums[0, :BLK], sums[1, :BLK]


def solution(mesh):
    in_specs = (
        P("dp", None),
        P(),
        P(),
        P(None, "dp", "tensor"),
        P("tensor", "dp"),
        P("dp", None),
        P(None, "tensor"),
        P("dp", "tensor"),
    )
    out_specs = (
        P("dp", "tensor"),
        P("dp", "tensor"),
        P(None, "dp", "tensor"),
        P("tensor", "dp"),
        P("tensor"),
        P("tensor"),
    )
    return jax.shard_map(local, mesh=mesh, in_specs=in_specs, out_specs=out_specs, check_vma=False)
```

time: 222 us -> 183 us (0.82); the launches traced: 219 us -> 183 us
  Pallas kernels: 195 us -> 174 us
  matrix products: 9.39 us -> 0 us
  other arithmetic: 2.82 us -> 0 us
  local copies, waits for them, and re-layouts: 11 us -> 8.74 us
    pallas_call x2 -> x1, Pallas kernels: 195 us -> 174 us  [sublayer(): pl.pallas_call(kernel, out_shape=[shape((BLK, SEQ), BF), shape((BLK, SEQ)...]
    dot_general x9 -> x0, matrix products: 9.39 us -> none  [the longest x3 3.16 us: attention_core(): jnp.einsum('qhd,khd->hqk', query, keys, preferred_element_type=jnp.float32)]
    unnamed x25 -> x4, local copies, waits for them, and re-layouts: 2.14 us -> 7.36 us
where the time goes in v2:
time: 183 us
  Pallas kernels  174 us (95%)
  local copies, waits for them, and re-layouts  8.74 us (5%)
    pallas_call x1, Pallas kernels, sublayer(): pl.pallas_call(kernel, out_shape=[shape((BLK, SEQ), BF), shape((BLK, SEQ)...  174 us
    unnamed x4, local copies, waits for them, and re-layouts  7.36 us

profile of v2, /device:TPU:1, one launch (start us, length us, event | category | flops | bytes accessed | tf_op | source)
XLA Modules:
  0.0 182.9 jit_solution(3594194224055434836)
XLA Ops:
  0.6 173.5 %shard_map.127 = (bf16[320,512]{1,0:T(8,128)(2,1)}, bf16[320,512]{1,0:T(8,128)(2,1)}, f32[3,320,256]{2,1,0:T(8,128)}, f32[320,256]{1,0:T(8,128)}, f32[8,384]{1,0:T(8,128)}) custom-call(bf16[512,5120]{1,0:T(8,128)(2,1)} %x_hbm.1, f32[1,5120]{1,0:T(1,128)} %bitcast.14, f32[1,5120]{1,0:T(1,128)} %bitcast.15, bf16[3,320,256]{2,1,0:T(8,128)(2,1)} %w_in.1, ...), custom_call_target="tpu_custom_call" | custom-call | tf_op jit(solution)/shard_map/pallas_call | solution.py:594
  174.2 1.4 slice_reduce_fusion
  175.6 1.7 copy.18
  177.3 1.7 copy.19
  179.0 2.2 %copy.20 = f32[3,320,256]{2,1,0:T(8,128)} copy(f32[3,320,256]{2,1,0:T(8,128)} %get-tuple-element.26) | data formatting | bytes 1966080
  181.2 1.7 copy.21

commit v3 on v2

v3 whole, which is shorter than its diff:
```python
import functools

import jax
import jax.numpy as jnp
from jax import lax
from jax.experimental import pallas as pl
from jax.experimental.pallas import tpu as pltpu
from jax.sharding import PartitionSpec as P

HDIM = 128
EPS = 1e-05
MESH = pl.DeviceIdType.MESH
F32, BF = jnp.float32, jnp.bfloat16

NZ, NY, NQ, NR = 8, 4, 8, 16
SEQ, D, C, W3 = 512, 5120, 640, 768
BLK = 320
SLAB = 640
HB = BLK // 2


def rem(a, n):
    return lax.rem(a, n)


def rows(start, size):
    return pl.ds(pl.multiple_of(start, 16), size)


def dot(a, b):
    return lax.dot_general(a, b, (((1,), (0,)), ((), ())), preferred_element_type=F32)


def dot_nt(a, b):
    return lax.dot_general(a, b, (((1,), (1,)), ((), ())), preferred_element_type=F32)


def dot_tn(a, b):
    return lax.dot_general(a, b, (((0,), (0,)), ((), ())), preferred_element_type=F32)


def remote(src, dst, ssem, rsem, **device):
    return pltpu.make_async_remote_copy(
        src_ref=src, dst_ref=dst, send_sem=ssem, recv_sem=rsem, device_id=device, device_id_type=MESH
    )


def enter():
    barrier = pltpu.get_barrier_semaphore()
    for axis in ("dp", "tensor"):
        me = lax.axis_index(axis)
        for k in range(1, NR):
            pl.semaphore_signal(barrier, inc=1, device_id={axis: rem(me + k, NR)}, device_id_type=MESH)
    dp, tensor = lax.axis_index("dp"), lax.axis_index("tensor")
    across = {"dp": dp + 1 - 2 * rem(dp, 2), "tensor": tensor + 1 - 2 * rem(tensor, 2)}
    pl.semaphore_signal(barrier, inc=1, device_id=across, device_id_type=MESH)
    pl.semaphore_wait(barrier, 2 * (NR - 1) + 1)


class Sum:
    def __init__(self, axis, part, out, buffers):
        self.axis, self.part, self.out = axis, part, out
        self.got, self.half, self.ring, self.mid, self.mid_got, self.ssem, self.rsem = buffers
        index = lax.axis_index(axis)
        self.n = self.ring.shape[0]
        self.a = rem(index, 2)
        self.q = rem(index // 2, self.n)
        self.top = index // (2 * self.n)
        self.h = part.shape[0] // 2
        self.b = self.h // self.n
        self.sent = []

    def at(self, top, q, a):
        return {self.axis: (top * self.n + q) * 2 + a}

    def pair(self):
        return self.at(self.top, self.q, 1 - self.a)

    def peer(self, k):
        return self.at(self.top, rem(self.q + k, self.n), self.a)

    def over(self):
        return self.at(1 - self.top, self.q, self.a)

    def go(self, copy):
        copy.start()
        self.sent.append(copy)

    def first(self):
        src = self.part.at[rows((1 - self.a) * self.h, self.h), :]
        self.go(remote(src, self.got, self.ssem.at[0], self.rsem.at[0], **self.pair()))

    def second(self):
        remote(self.got, self.got, self.ssem.at[0], self.rsem.at[0], **self.pair()).wait_recv()
        mine = self.part[rows(self.a * self.h, self.h), :].astype(F32)
        self.half[...] = (mine + self.got[...].astype(F32)).astype(BF)
        for k in range(1, self.n):
            to = rem(self.q + k, self.n)
            src = self.half.at[rows(to * self.b, self.b), :]
            self.go(remote(src, self.ring.at[self.q], self.ssem.at[k], self.rsem.at[k], **self.peer(k)))

    def reduced(self):
        total = self.half[rows(self.q * self.b, self.b), :].astype(F32)
        for k in range(1, self.n):
            source = rem(self.q + self.n - k, self.n)
            slot = self.ring.at[source]
            remote(slot, slot, self.ssem.at[k], self.rsem.at[k], **self.peer(k)).wait_recv()
            total = total + self.ring[source].astype(F32)
        return total

    def spread(self, total):
        here = rows(self.a * self.h + self.q * self.b, self.b)
        self.out[here, :] = total.astype(BF)
        piece = self.out.at[here, :]
        for k in range(1, self.n):
            self.go(remote(piece, piece, self.ssem.at[7 + k], self.rsem.at[7 + k], **self.peer(k)))

    def third(self):
        if self.mid is None:
            self.spread(self.reduced())
        else:
            self.mid[...] = self.reduced().astype(BF)
            self.go(remote(self.mid, self.mid_got, self.ssem.at[16], self.rsem.at[16], **self.over()))

    def across(self):
        remote(self.mid, self.mid_got, self.ssem.at[16], self.rsem.at[16], **self.over()).wait_recv()
        self.spread(self.mid[...].astype(F32) + self.mid_got[...].astype(F32))

    def fourth(self):
        for k in range(1, self.n):
            source = rem(self.q + self.n - k, self.n)
            piece = self.out.at[rows(self.a * self.h + source * self.b, self.b), :]
            remote(piece, piece, self.ssem.at[7 + k], self.rsem.at[7 + k], **self.peer(k)).wait_recv()
        mine = self.out.at[rows(self.a * self.h, self.h), :]
        self.go(remote(mine, mine, self.ssem.at[15], self.rsem.at[15], **self.pair()))

    def last(self):
        other = self.out.at[rows((1 - self.a) * self.h, self.h), :]
        remote(other, other, self.ssem.at[15], self.rsem.at[15], **self.pair()).wait_recv()

    def drain(self):
        for copy in self.sent:
            copy.wait_send()


def dma(*shape):
    return pltpu.SemaphoreType.DMA(shape)


def sum_buffers(r, n):
    h = r // 2
    cut = pltpu.VMEM((h // n, C), BF)
    mids = [cut, cut] if n == NY else [None, None]
    return [pltpu.VMEM((h, C), BF), pltpu.VMEM((h, C), BF), pltpu.VMEM((n, h // n, C), BF)] + mids + [dma(17), dma(17)]


def add_rows(dst, src):
    @pl.loop(0, dst.shape[0] // 80)
    def _(i):
        here = rows(i * 80, 80)
        dst[here, :] = (dst[here, :].astype(F32) + src[here, :].astype(F32)).astype(BF)


def kernel(
    x_hbm, gain, bias, w_in, owt, enc, dect, got,
    ro_t, gi_t, gq, gow_t, gb,
    x, w, nb, no, acc, mu, rstd, xt, gcol, hat, st,
    cg_part, fo_part, cg, folded, ps, pr, qkvt, qkv, ag, attn, qg, qo, qgt, dkv,
    con, rb1, rb, po, px, cr, ys, yr, xs, xv, fs, fv, ng, lt, gs, cp_part, mx_part, code, mixing,
    t1, d1, t2, d2,
    x_sem, loc, a_ss, a_rs, n_ss, n_rs, f_ss, f_rs, p_ss, p_rs, q_ss, q_rs,
    r1_ss, r1_rs, r_ss, r_rs, cs_ss, cs_rs, y_ss, y_rs, xh_ss, xh_rs, fs_ss, fs_rs, lt_ss, lt_rs, gs_ss, gs_rs,
):
    dp, tensor = lax.axis_index("dp"), lax.axis_index("tensor")
    z, xl = dp // 2, rem(dp, 2)
    up, down = rem(z + 1, NZ) * 2 + xl, rem(z + NZ - 1, NZ) * 2 + xl
    other = z * 2 + 1 - xl
    core, q = rem(tensor, 2), tensor // 2
    xh, y = q // NY, rem(q, NY)
    sibling = q * 2 + 1 - core
    ways = ((0, up), (1, down))
    sent = []

    def go(copy):
        copy.start()
        sent.append(copy)

    x_copies = [
        pltpu.make_async_copy(x_hbm.at[pl.ds(i * 128, 128), :], x.at[pl.ds(i * 128, 128), :], x_sem.at[i])
        for i in range(4)
    ]
    for copy in x_copies:
        copy.start()
    enter()

    def block(j, zs, offset=0, size=BLK):
        return w.at[j, rows(zs * BLK + offset, size), :]

    mine = pltpu.make_async_copy(w_in, w.at[:, rows(z * BLK, BLK), :], loc)
    mine.start()

    def send_own(j):
        for way, to in ways:
            go(remote(w_in.at[j], block(j, z), a_ss.at[way, j, 0], a_rs.at[way, j, 0], dp=to))

    def relay(j, s):
        for way, to in ways:
            zs = rem(z + (NZ - s if way == 0 else s), NZ)
            if s < 4:
                part = block(j, zs)
                remote(part, part, a_ss.at[way, j, s - 1], a_rs.at[way, j, s - 1], dp=to).wait_recv()
                if s == 3:
                    part = block(j, zs, way * HB, HB)
                go(remote(part, part, a_ss.at[way, j, s], a_rs.at[way, j, s], dp=to))
            else:
                part = block(j, zs, way * HB, HB)
                remote(part, part, a_ss.at[way, j, 3], a_rs.at[way, j, 3], dp=to).wait_recv()

    send_own(0)
    send_own(1)
    fo_part[...] = dot_tn(owt[...], enc[...]).astype(BF)
    sum_d = Sum("dp", fo_part, folded, d1)
    sum_d.first()

    def slab_cols(zs):
        return pl.ds(pl.multiple_of(zs * SLAB, 128), SLAB)

    def near(i):
        odd = rem(i, 2)
        return rem(z + odd * ((i + 1) // 2) + (1 - odd) * (NZ - i // 2), NZ)

    def tokens(r):
        return pl.ds(r * 128, 128)

    def cross(k, r):
        zs = near(2 * k + core)
        src, dst = nb.at[1, zs, :, tokens(r)], no.at[zs, :, tokens(r)]
        return remote(src, dst, n_ss.at[k, r], n_rs.at[k, r], dp=other)

    def pass_on(k, r):
        part = no.at[near(2 * k + core), :, tokens(r)]
        return remote(part, part, f_ss.at[k, r], f_rs.at[k, r], tensor=sibling)

    def norm(r):
        x_copies[r].wait()
        xt[:, r * 128 : (r + 1) * 128] = x[r * 128 : (r + 1) * 128, slab_cols(q)].T

        @pl.loop(0, 8)
        def _(i):
            here = rows(r * 128 + i * 16, 16)
            v = x[here, :].astype(F32)
            mean = jnp.sum(v, axis=1, keepdims=True) * (1.0 / D)
            v = v - mean
            var = jnp.sum(v * v, axis=1, keepdims=True) * (1.0 / D)
            scale = lax.rsqrt(var + EPS)
            mu[here, :] = jnp.broadcast_to(mean, (16, 128))
            rstd[here, :] = jnp.broadcast_to(scale, (16, 128))
            x[here, :] = (v * scale * gain[...] + bias[...]).astype(BF)

        @pl.loop(0, NZ)
        def _(zs):
            v = x[r * 128 : (r + 1) * 128, slab_cols(zs)].T
            nb[xl, zs, :, r * 128 : (r + 1) * 128] = v[0:BLK]
            nb[1 - xl, zs, :, r * 128 : (r + 1) * 128] = v[BLK:SLAB]

        for k in range(4):
            go(cross(k, r))

    def forward_on(r):
        for k in range(4):
            cross(k, r).wait_recv()
            go(pass_on(k, r))

    def use(j, i, part):
        zs = near(i)
        here = slice(j * 256, (j + 1) * 256)
        source = nb.at[0, zs] if part == 0 else no.at[zs]
        acc[part, here, :] += dot_tn(block(j, zs)[...], source[...])

    def use_all(j, lo, hi, part):
        @pl.loop(lo, hi)
        def _(i):
            use(j, i, part)

    acc[...] = jnp.zeros_like(acc)
    norm(0)
    relay(0, 1)
    norm(1)
    relay(1, 1)
    sum_d.second()
    cg_part[...] = dot_tn(got[...], dect[...]).astype(BF)
    sum_t = Sum("tensor", cg_part, cg, t1)
    sum_t.first()
    relay(0, 2)
    norm(2)
    relay(1, 2)
    forward_on(0)
    norm(3)
    relay(0, 3)
    send_own(2)
    sum_t.second()
    forward_on(1)
    mine.wait()
    sum_d.third()
    use_all(0, 0, 5, 0)
    relay(1, 3)
    sum_t.third()
    use_all(1, 0, 5, 0)
    relay(2, 1)
    relay(0, 4)
    forward_on(2)
    sum_d.fourth()
    sum_t.across()
    use_all(0, 5, 8, 0)
    relay(2, 2)
    use_all(1, 5, 7, 0)
    relay(1, 4)
    use_all(1, 7, 8, 0)
    sum_t.fourth()
    forward_on(3)
    use_all(2, 0, 5, 0)
    relay(2, 3)
    for r in range(4):
        for k in range(4):
            part = no.at[near(2 * k + 1 - core), :, tokens(r)]
            remote(part, part, f_ss.at[k, r], f_rs.at[k, r], tensor=sibling).wait_recv()

    def partial(j):
        here = pl.ds(j * 256, 256)
        return remote(ps.at[here, :], pr.at[here, :], p_ss.at[j], p_rs.at[j], dp=other)

    def give(j):
        here = slice(j * 256, (j + 1) * 256)
        ps[here, :] = acc[1, here, :].astype(BF)
        go(partial(j))

    def take(j):
        here = slice(j * 256, (j + 1) * 256)
        partial(j).wait_recv()
        qkvt[here, :] = (acc[0, here, :] + pr[here, :].astype(F32)).astype(BF)
        qkv[:, here] = qkvt[here, :].T

    use_all(0, 0, 8, 1)
    give(0)
    relay(2, 4)
    use_all(1, 0, 8, 1)
    give(1)
    use_all(2, 0, 8, 1)
    give(2)
    sum_d.last()
    sum_t.last()
    use_all(2, 5, 8, 0)
    ag[...] = dot_nt(cg[...], folded[...]).astype(BF)
    mine_rows = rows(core * BLK, BLK)
    rs_row = rstd[...].T[0:1, :]
    hat[...] = (xt[mine_rows, :].astype(F32) - mu[...].T[0:1, :]) * rs_row
    st[0:1, :] = rs_row
    gcol[...] = jnp.broadcast_to(gain[0:1, slab_cols(q)], (128, SLAB)).T
    dkv[...] = jnp.zeros_like(dkv)
    for j in range(3):
        take(j)

    rate = HDIM**-0.5
    for h in range(2):
        cq = slice(h * HDIM, (h + 1) * HDIM)
        ck = slice(256 + h * HDIM, 256 + (h + 1) * HDIM)
        cv = slice(512 + h * HDIM, 512 + (h + 1) * HDIM)
        for r in range(4):
            here, n = slice(r * 128, (r + 1) * 128), 128 * (r + 1)
            qb, kb, vb = qkv[here, cq], qkv[0:n, ck], qkv[0:n, cv]
            s = dot_nt(qb, kb) * rate
            at_row = lax.broadcasted_iota(jnp.int32, (128, n), 0) + r * 128
            at_col = lax.broadcasted_iota(jnp.int32, (128, n), 1)
            s = jnp.where(at_col <= at_row, s, -1e30)
            e = jnp.exp(s - jnp.max(s, axis=1, keepdims=True))
            p = e * (1.0 / jnp.sum(e, axis=1, keepdims=True))
            pb = p.astype(BF)
            attn[here, cq] = dot(pb, vb).astype(BF)
            da = ag[here, cq]
            dpr = dot_nt(da, vb).astype(BF).astype(F32)
            ds = p * (dpr - jnp.sum(p * dpr, axis=1, keepdims=True))
            ds = (ds * rate).astype(BF)
            qg[here, cq] = dot(ds, kb).astype(BF)
            dkv[0:n, cq] += dot_tn(ds, qb)
            dkv[0:n, ck] += dot_tn(pb, da)
    qg[:, 256:768] = dkv[...].astype(BF)

    def swap_grad(j):
        here = pl.ds(j * 256, 256)
        return remote(qg.at[:, here], qo.at[:, here], q_ss.at[j], q_rs.at[j], dp=other)

    for j in (2, 0, 1):
        go(swap_grad(j))

    def contribute(zs):
        for j in range(3):
            con[zs, j] = dot(nb[0, zs], qg[:, j * 256 : (j + 1) * 256]).astype(BF)

    @pl.loop(0, NZ)
    def _(zs):
        contribute(zs)

    def turn(part, source):
        @pl.loop(0, 6)
        def _(i):
            here = pl.ds(pl.multiple_of(i * 128, 128), 128)
            qgt[part, here, :] = source[:, here].T

    turn(0, qg)

    def term(zs, part):
        here = rows(zs * BLK, BLK)
        out = dot(w[0, here, :], qgt[part, 0:256, :])
        out = out + dot(w[1, here, :], qgt[part, 256:512, :])
        return out + dot(w[2, here, :], qgt[part, 512:768, :])

    def feature(i):
        return rem(i, 2) * NY + rem(y + 1 + i // 2, NY)

    keeps = core == xl

    def to_core(buffer, i):
        return remote(buffer.at[i], cr.at[i], cs_ss.at[i], cs_rs.at[i], tensor=sibling)

    def to_y(i):
        there = (xh * NY + rem(y + 1 + i // 2, NY)) * 2 + core
        return remote(ys.at[i], yr.at[i], y_ss.at[i], y_rs.at[i], tensor=there)

    def parts(buffer, part):
        @pl.loop(0, NQ)
        def _(i):
            buffer[i] = term(feature(i), part).astype(BF)

    def pass_core(buffer):
        @pl.loop(0, NQ)
        def _(i):
            to_core(buffer, i).start()

    def join(buffer):
        def one(i):
            to_core(buffer, i).wait_recv()
            ys[i] = (buffer[i].astype(F32) + cr[i].astype(F32)).astype(BF)

        @pl.loop(0, NQ - 2)
        def _(i):
            one(i)
            to_y(i).start()

        @pl.loop(NQ - 2, NQ)
        def _(i):
            one(i)

    parts(po, 0)

    @pl.when(jnp.logical_not(keeps))
    def _():
        pass_core(po)

    def complete(j):
        swap_grad(j).wait_recv()

        @pl.loop(0, NZ)
        def _(zs):
            here = slice(j * 256, (j + 1) * 256)
            con[zs, j] = (con[zs, j].astype(F32) + dot(no[zs], qo[:, here])).astype(BF)

    def ring(j, s):
        for way, to in ways:
            if s == 1:
                half = con.at[rem(z + 4, NZ), j, pl.ds(way * HB, HB), :]
                go(remote(half, rb1.at[j, way], r1_ss.at[j, way], r1_rs.at[j, way], dp=to))
                continue
            zs = rem(z + (5 - s if way == 0 else NZ + s - 5), NZ)
            if s == 2:
                remote(rb1.at[j, way], rb1.at[j, way], r1_ss.at[j, way], r1_rs.at[j, way], dp=to).wait_recv()
                add_rows(con.at[zs, j, pl.ds(way * HB, HB), :], rb1.at[j, way])
            else:
                slot = rb.at[j, way, s - 3]
                remote(slot, slot, r_ss.at[j, way, s - 3], r_rs.at[j, way, s - 3], dp=to).wait_recv()
                add_rows(con.at[zs, j], slot)
            if s < 5:
                slot = rb.at[j, way, s - 2]
                go(remote(con.at[zs, j], slot, r_ss.at[j, way, s - 2], r_rs.at[j, way, s - 2], dp=to))
        if s == 5:
            gq[j] = con[z, j].astype(F32) * (1.0 / NR)

    complete(2)
    ring(2, 1)
    cp_part[...] = dot(attn[...], folded[...]).astype(BF)
    sum_t2 = Sum("tensor", cp_part, code, t2)
    sum_t2.first()
    mx_part[...] = dot_tn(attn[...], cg[...]).astype(BF)
    sum_d2 = Sum("dp", mx_part, mixing, d2)
    sum_d2.first()
    ring(2, 2)
    complete(0)
    ring(0, 1)

    @pl.when(keeps)
    def _():
        join(po)

    ring(2, 3)
    ring(0, 2)
    complete(1)
    ring(1, 1)
    turn(1, qo)
    parts(px, 1)

    @pl.when(keeps)
    def _():
        pass_core(px)

    ring(2, 4)
    ring(0, 3)
    ring(1, 2)

    @pl.when(jnp.logical_not(keeps))
    def _():
        join(px)

    sum_t2.second()
    sum_d2.second()
    ring(2, 5)
    ring(0, 4)
    ring(1, 3)
    sum_t2.third()

    for i in range(NQ - 2):
        remote(yr.at[i], yr.at[i], y_ss.at[i], y_rs.at[i], tensor=tensor).wait_recv()

    def y_sum(which):
        total = ys[6 + which].astype(F32)
        for k in range(3):
            total = total + yr[2 * k + which].astype(F32)
        return total

    xs[...] = y_sum(1 - xh).astype(BF)
    swap = remote(xs, xv, xh_ss, xh_rs, tensor=((1 - xh) * NY + y) * 2 + core)
    swap.start()
    ng[...] = y_sum(xh)
    sum_d2.third()
    ring(0, 5)
    ring(1, 4)
    sum_t2.across()
    swap.wait_recv()
    ng[...] = ng[...] + xv[...].astype(F32)
    home = remote(fs, fv, fs_ss, fs_rs, dp=other, tensor=sibling)

    @pl.when(jnp.logical_not(keeps))
    def _():
        fs[...] = ng[...].astype(BF)
        home.start()
        home.wait_recv()
        ng[...] = fv[...].astype(F32)

    grad = ng[...]
    scaled = grad * gcol[mine_rows, 0:1]
    lt[tensor, 0:1, :] = jnp.sum(scaled, axis=0, keepdims=True)
    lt[tensor, 1:2, :] = jnp.sum(scaled * hat[...], axis=0, keepdims=True)
    slot = lt.at[tensor]
    for k in range(1, NR):
        go(remote(slot, slot, lt_ss.at[k], lt_rs.at[k], tensor=rem(tensor + k, NR)))

    def fold(v):
        v = v[:, 0:128] + v[:, 128:256] + v[:, 256:384] + v[:, 384:512]
        v = jnp.concatenate([v, jnp.zeros((64, 128), F32)], axis=0)
        return jnp.sum(v.T, axis=0, keepdims=True)

    gs[dp, 0:1, :] = fold(ng[...] * hat[...])
    gs[dp, 1:2, :] = fold(ng[...])
    slot = gs.at[dp]
    for k in range(1, NR):
        go(remote(slot, slot, gs_ss.at[k], gs_rs.at[k], dp=rem(dp + k, NR)))
    sum_d2.fourth()
    sum_t2.fourth()
    ring(1, 5)
    sum_t2.last()
    ro_t[...] = (xt[mine_rows, :].astype(F32) + dot_nt(dect[...], code[...])).astype(BF)

    for k in range(1, NR):
        slot = lt.at[rem(tensor + NR - k, NR)]
        remote(slot, slot, lt_ss.at[k], lt_rs.at[k], tensor=tensor).wait_recv()
    sums = jnp.sum(lt[...], axis=0)
    lead, trail = sums[0:1, :] * (1.0 / D), sums[1:2, :] * (1.0 / D)
    scaled = ng[...] * gcol[mine_rows, 0:1]
    gi_t[...] = (got[...].astype(F32) + st[0:1, :] * (scaled - lead - hat[...] * trail)).astype(BF)
    sum_d2.last()
    gow_t[...] = dot_nt(enc[...], mixing[...]) * (1.0 / NR)
    for k in range(1, NR):
        slot = gs.at[rem(dp + NR - k, NR)]
        remote(slot, slot, gs_ss.at[k], gs_rs.at[k], dp=dp).wait_recv()
    gb[...] = jnp.sum(gs[...], axis=0) * (1.0 / NR)

    for total in (sum_t, sum_d, sum_t2, sum_d2):
        total.drain()
    swap.wait_send()
    for copy in sent:
        copy.wait_send()

    @pl.when(jnp.logical_not(keeps))
    def _():
        home.wait_send()

    @pl.loop(0, NQ)
    def _(i):
        to_core(po, i).wait_send()

    @pl.loop(0, NQ - 2)
    def _(i):
        to_y(i).wait_send()


def sublayer(*args):
    def shape(dims, kind):
        return jax.ShapeDtypeStruct(dims, kind)

    def v(kind, *dims):
        return pltpu.VMEM(dims, kind)

    one = pltpu.SemaphoreType.DMA
    whole = pl.BlockSpec(memory_space=pltpu.VMEM)
    far = pl.BlockSpec(memory_space=pl.ANY)
    scratch = [
        v(BF, SEQ, D), v(BF, 3, NZ * BLK, 256), v(BF, 2, NZ, BLK, SEQ), v(BF, NZ, BLK, SEQ), v(F32, 2, W3, SEQ),
        v(F32, SEQ, 128), v(F32, SEQ, 128), v(BF, SLAB, SEQ), v(F32, SLAB, 128), v(F32, BLK, SEQ), v(F32, 8, SEQ),
        v(BF, SEQ, C), v(BF, 256, C), v(BF, SEQ, C), v(BF, 256, C), v(BF, W3, SEQ), v(BF, W3, SEQ), v(BF, W3, SEQ),
        v(BF, SEQ, W3), v(BF, SEQ, 256), v(BF, SEQ, 256), v(BF, SEQ, W3), v(BF, SEQ, W3), v(BF, 2, W3, SEQ),
        v(F32, SEQ, 512),
        v(BF, NZ, 3, BLK, 256), v(BF, 3, 2, HB, 256), v(BF, 3, 2, 3, BLK, 256),
        v(BF, NQ, BLK, SEQ), v(BF, NQ, BLK, SEQ), v(BF, NQ, BLK, SEQ), v(BF, NQ, BLK, SEQ), v(BF, NQ - 2, BLK, SEQ),
        v(BF, BLK, SEQ), v(BF, BLK, SEQ), v(BF, BLK, SEQ), v(BF, BLK, SEQ), v(F32, BLK, SEQ),
        v(F32, NR, 8, SEQ), v(F32, NR, 8, 384), v(BF, SEQ, C), v(BF, 256, C), v(BF, SEQ, C), v(BF, 256, C),
        sum_buffers(SEQ, NY), sum_buffers(256, NZ), sum_buffers(SEQ, NY), sum_buffers(256, NZ),
        dma(4), one, dma(2, 3, 4), dma(2, 3, 4), dma(4, 4), dma(4, 4), dma(4, 4), dma(4, 4), dma(3), dma(3), dma(3), dma(3),
        dma(3, 2), dma(3, 2), dma(3, 2, 3), dma(3, 2, 3), dma(NQ), dma(NQ), dma(NQ), dma(NQ), one, one, one, one,
        dma(NR), dma(NR), dma(NR), dma(NR),
    ]
    return pl.pallas_call(
        kernel,
        out_shape=[
            shape((BLK, SEQ), BF),
            shape((BLK, SEQ), BF),
            shape((3, BLK, 256), F32),
            shape((BLK, 256), F32),
            shape((8, 384), F32),
        ],
        in_specs=[far, whole, whole, far, whole, whole, whole, whole],
        out_specs=[whole] * 5,
        scratch_shapes=scratch,
        compiler_params=pltpu.CompilerParams(
            collective_id=0, has_side_effects=True, vmem_limit_bytes=62 * 2**20
        ),
    )(*args)


def local(
    residual_in,
    layernorm_gain,
    layernorm_bias,
    qkv_weight,
    out_weight,
    encoder,
    decoder,
    grad_output,
):
    residual_out, grad_input, grad_qkv, grad_out_weight, sums = sublayer(
        residual_in,
        layernorm_gain[None, :],
        layernorm_bias[None, :],
        qkv_weight,
        out_weight.T,
        encoder,
        decoder.T,
        grad_output.T,
    )
    return residual_out.T, grad_input.T, grad_qkv, grad_out_weight.T, sums[0, :BLK], sums[1, :BLK]


def solution(mesh):
    in_specs = (
        P("dp", None),
        P(),
        P(),
        P(None, "dp", "tensor"),
        P("tensor", "dp"),
        P("dp", None),
        P(None, "tensor"),
        P("dp", "tensor"),
    )
    out_specs = (
        P("dp", "tensor"),
        P("dp", "tensor"),
        P(None, "dp", "tensor"),
        P("tensor", "dp"),
        P("tensor"),
        P("tensor"),
    )
    return jax.shard_map(local, mesh=mesh, in_specs=in_specs, out_specs=out_specs, check_vma=False)
```

time: 183 us -> 174 us (0.951)
  Pallas kernels: 174 us -> 164 us
    pallas_call x1, Pallas kernels: 174 us -> 164 us  [sublayer(): pl.pallas_call(kernel, out_shape=[shape((BLK, SEQ), BF), shape((BLK, SEQ)...]
where the time goes in v3:
time: 174 us
  Pallas kernels  164 us (94%)
  local copies, waits for them, and re-layouts  8.74 us (5%)
    pallas_call x1, Pallas kernels, sublayer(): pl.pallas_call(kernel, out_shape=[shape((BLK, SEQ), BF), shape((BLK, SEQ)...  164 us
    unnamed x4, local copies, waits for them, and re-layouts  7.36 us

profile of v3, /device:TPU:1, one launch (start us, length us, event | category | flops | bytes accessed | tf_op | source)
XLA Modules:
  0.0 173.6 jit_solution(7015232032798508251)
XLA Ops:
  0.6 164.2 %shard_map.127 = (bf16[320,512]{1,0:T(8,128)(2,1)}, bf16[320,512]{1,0:T(8,128)(2,1)}, f32[3,320,256]{2,1,0:T(8,128)}, f32[320,256]{1,0:T(8,128)}, f32[8,384]{1,0:T(8,128)}) custom-call(bf16[512,5120]{1,0:T(8,128)(2,1)} %x_hbm.1, f32[1,5120]{1,0:T(1,128)} %bitcast.14, f32[1,5120]{1,0:T(1,128)} %bitcast.15, bf16[3,320,256]{2,1,0:T(8,128)(2,1)} %w_in.1, ...), custom_call_target="tpu_custom_call" | custom-call | tf_op jit(solution)/shard_map/pallas_call | solution.py:639
  164.9 1.4 slice_reduce_fusion
  166.2 1.7 copy.18
  168.0 1.7 copy.19
  169.7 2.2 %copy.20 = f32[3,320,256]{2,1,0:T(8,128)} copy(f32[3,320,256]{2,1,0:T(8,128)} %get-tuple-element.26) | data formatting | bytes 1966080
  171.9 1.7 copy.21

commit v4 on v3

--- a/solution.py
+++ b/solution.py
@@ -1,4 +1,5 @@
 import functools
+from collections import deque
 
 import jax
 import jax.numpy as jnp
@@ -166,10 +167,10 @@
     ro_t, gi_t, gq, gow_t, gb,
     x, w, nb, no, acc, mu, rstd, xt, gcol, hat, st,
     cg_part, fo_part, cg, folded, ps, pr, qkvt, qkv, ag, attn, qg, qo, qgt, dkv,
-    con, rb1, rb, po, px, cr, ys, yr, xs, xv, fs, fv, ng, lt, gs, cp_part, mx_part, code, mixing,
+    con, rb1, rb, po, px, cr, ys, yh, yr, xs, xv, fs, fv, ng, lt, gs, cp_part, mx_part, code, mixing,
     t1, d1, t2, d2,
     x_sem, loc, a_ss, a_rs, n_ss, n_rs, f_ss, f_rs, p_ss, p_rs, q_ss, q_rs,
-    r1_ss, r1_rs, r_ss, r_rs, cs_ss, cs_rs, y_ss, y_rs, xh_ss, xh_rs, fs_ss, fs_rs, lt_ss, lt_rs, gs_ss, gs_rs,
+    r1_ss, r1_rs, r_ss, r_rs, cs_ss, cs_rs, yh_ss, yh_rs, y_ss, y_rs, xh_ss, xh_rs, fs_ss, fs_rs, lt_ss, lt_rs, gs_ss, gs_rs,
 ):
     dp, tensor = lax.axis_index("dp"), lax.axis_index("tensor")
     z, xl = dp // 2, rem(dp, 2)
@@ -218,9 +219,16 @@
 
     send_own(0)
     send_own(1)
-    fo_part[...] = dot_tn(owt[...], enc[...]).astype(BF)
     sum_d = Sum("dp", fo_part, folded, d1)
-    sum_d.first()
+    sum_t = Sum("tensor", cg_part, cg, t1)
+
+    def start_folded():
+        fo_part[...] = dot_tn(owt[...], enc[...]).astype(BF)
+        sum_d.first()
+
+    def start_code_grad():
+        cg_part[...] = dot_tn(got[...], dect[...]).astype(BF)
+        sum_t.first()
 
     def slab_cols(zs):
         return pl.ds(pl.multiple_of(zs * SLAB, 128), SLAB)
@@ -241,11 +249,12 @@
         part = no.at[near(2 * k + core), :, tokens(r)]
         return remote(part, part, f_ss.at[k, r], f_rs.at[k, r], tensor=sibling)
 
-    def norm(r):
-        x_copies[r].wait()
-        xt[:, r * 128 : (r + 1) * 128] = x[r * 128 : (r + 1) * 128, slab_cols(q)].T
-
-        @pl.loop(0, 8)
+    def norm(r, lo, hi):
+        if lo == 0:
+            x_copies[r].wait()
+            xt[:, r * 128 : (r + 1) * 128] = x[r * 128 : (r + 1) * 128, slab_cols(q)].T
+
+        @pl.loop(lo, hi)
         def _(i):
             here = rows(r * 128 + i * 16, 16)
             v = x[here, :].astype(F32)
@@ -257,6 +266,7 @@
             rstd[here, :] = jnp.broadcast_to(scale, (16, 128))
             x[here, :] = (v * scale * gain[...] + bias[...]).astype(BF)
 
+    def spread(r):
         @pl.loop(0, NZ)
         def _(zs):
             v = x[r * 128 : (r + 1) * 128, slab_cols(zs)].T
@@ -282,49 +292,6 @@
         def _(i):
             use(j, i, part)
 
-    acc[...] = jnp.zeros_like(acc)
-    norm(0)
-    relay(0, 1)
-    norm(1)
-    relay(1, 1)
-    sum_d.second()
-    cg_part[...] = dot_tn(got[...], dect[...]).astype(BF)
-    sum_t = Sum("tensor", cg_part, cg, t1)
-    sum_t.first()
-    relay(0, 2)
-    norm(2)
-    relay(1, 2)
-    forward_on(0)
-    norm(3)
-    relay(0, 3)
-    send_own(2)
-    sum_t.second()
-    forward_on(1)
-    mine.wait()
-    sum_d.third()
-    use_all(0, 0, 5, 0)
-    relay(1, 3)
-    sum_t.third()
-    use_all(1, 0, 5, 0)
-    relay(2, 1)
-    relay(0, 4)
-    forward_on(2)
-    sum_d.fourth()
-    sum_t.across()
-    use_all(0, 5, 8, 0)
-    relay(2, 2)
-    use_all(1, 5, 7, 0)
-    relay(1, 4)
-    use_all(1, 7, 8, 0)
-    sum_t.fourth()
-    forward_on(3)
-    use_all(2, 0, 5, 0)
-    relay(2, 3)
-    for r in range(4):
-        for k in range(4):
-            part = no.at[near(2 * k + 1 - core), :, tokens(r)]
-            remote(part, part, f_ss.at[k, r], f_rs.at[k, r], tensor=sibling).wait_recv()
-
     def partial(j):
         here = pl.ds(j * 256, 256)
         return remote(ps.at[here, :], pr.at[here, :], p_ss.at[j], p_rs.at[j], dp=other)
@@ -340,16 +307,86 @@
         qkvt[here, :] = (acc[0, here, :] + pr[here, :].astype(F32)).astype(BF)
         qkv[:, here] = qkvt[here, :].T
 
-    use_all(0, 0, 8, 1)
-    give(0)
-    relay(2, 4)
-    use_all(1, 0, 8, 1)
-    give(1)
-    use_all(2, 0, 8, 1)
-    give(2)
+    def collect():
+        for r in range(4):
+            for k in range(4):
+                part = no.at[near(2 * k + 1 - core), :, tokens(r)]
+                remote(part, part, f_ss.at[k, r], f_rs.at[k, r], tensor=sibling).wait_recv()
+
+    work = deque()
+
+    def add(cost, f, *args):
+        work.append((cost, functools.partial(f, *args)))
+
+    def clear():
+        acc[...] = jnp.zeros_like(acc)
+
+    def relay_use(j, s):
+        relay(j, s)
+        lo, hi = (7, 8) if s == 4 else (2 * s - 1, 2 * s + 1)
+        add(0.33 * (hi - lo), use_all, j, lo, hi, 0)
+
+    def own_use():
+        mine.wait()
+        for j in range(3):
+            add(0.33, use_all, j, 0, 1, 0)
+
+    def far_use(j):
+        use_all(j, 0, 8, 1)
+        give(j)
+
+    add(1.2, start_folded)
+    for r in range(4):
+        add(1.3, norm, r, 0, 4)
+        add(1.3, norm, r, 4, 8)
+        add(1.1, spread, r)
+        if r == 0:
+            add(0.8, clear)
+        if r == 2:
+            add(1.5, start_code_grad)
+    events = [
+        (5.0, relay_use, 0, 1),
+        (7.0, sum_d.second),
+        (8.3, relay_use, 1, 1),
+        (11.6, relay_use, 0, 2),
+        (13.5, forward_on, 0),
+        (16.5, relay_use, 1, 2),
+        (16.6, send_own, 2),
+        (19.0, sum_d.third),
+        (20.0, relay_use, 0, 3),
+        (20.5, forward_on, 1),
+        (21.0, own_use),
+        (21.5, sum_t.second),
+        (24.0, relay_use, 2, 1),
+        (25.5, sum_t.third),
+        (28.0, relay_use, 1, 3),
+        (28.0, forward_on, 2),
+        (29.5, sum_t.across),
+        (31.0, relay_use, 0, 4),
+        (31.5, sum_d.fourth),
+        (34.0, relay_use, 2, 2),
+        (34.2, sum_t.fourth),
+        (35.0, forward_on, 3),
+        (36.0, relay_use, 1, 4),
+        (37.5, collect),
+        (38.0, far_use, 0),
+        (39.5, relay_use, 2, 3),
+        (40.0, far_use, 1),
+        (43.0, relay_use, 2, 4),
+        (43.0, far_use, 2),
+    ]
+    now = 0.0
+    for when, f, *args in events:
+        while work and now + work[0][0] <= when + 0.3:
+            cost, g = work.popleft()
+            g()
+            now += cost
+        f(*args)
+        now = max(now, when) + (2.8 if f is far_use else 0.2)
+    while work:
+        work.popleft()[1]()
     sum_d.last()
     sum_t.last()
-    use_all(2, 5, 8, 0)
     ag[...] = dot_nt(cg[...], folded[...]).astype(BF)
     mine_rows = rows(core * BLK, BLK)
     rs_row = rstd[...].T[0:1, :]
@@ -392,13 +429,10 @@
     for j in (2, 0, 1):
         go(swap_grad(j))
 
-    def contribute(zs):
-        for j in range(3):
+    def contribute(j):
+        @pl.loop(0, NZ)
+        def _(zs):
             con[zs, j] = dot(nb[0, zs], qg[:, j * 256 : (j + 1) * 256]).astype(BF)
-
-    @pl.loop(0, NZ)
-    def _(zs):
-        contribute(zs)
 
     def turn(part, source):
         @pl.loop(0, 6)
@@ -406,8 +440,6 @@
             here = pl.ds(pl.multiple_of(i * 128, 128), 128)
             qgt[part, here, :] = source[:, here].T
 
-    turn(0, qg)
-
     def term(zs, part):
         here = rows(zs * BLK, BLK)
         out = dot(w[0, here, :], qgt[part, 0:256, :])
@@ -415,49 +447,78 @@
         return out + dot(w[2, here, :], qgt[part, 512:768, :])
 
     def feature(i):
-        return rem(i, 2) * NY + rem(y + 1 + i // 2, NY)
+        return i % 2 * NY + rem(y + (2, 1, 3, 0)[i // 2], NY)
 
     keeps = core == xl
 
     def to_core(buffer, i):
         return remote(buffer.at[i], cr.at[i], cs_ss.at[i], cs_rs.at[i], tensor=sibling)
 
-    def to_y(i):
-        there = (xh * NY + rem(y + 1 + i // 2, NY)) * 2 + core
-        return remote(ys.at[i], yr.at[i], y_ss.at[i], y_rs.at[i], tensor=there)
-
-    def parts(buffer, part):
-        @pl.loop(0, NQ)
-        def _(i):
+    def y_device(way):
+        return (xh * NY + rem(y + 1 + 2 * way, NY)) * 2 + core
+
+    def y_half(way, side):
+        src = ys.at[side, pl.ds(way * HB, HB), :]
+        return remote(src, yh.at[way, side], yh_ss.at[way, side], yh_rs.at[way, side], tensor=y_device(way))
+
+    def y_full(way, side):
+        src = ys.at[2 + 2 * way + side]
+        return remote(src, yr.at[way, side], y_ss.at[way, side], y_rs.at[way, side], tensor=y_device(way))
+
+    def join(buffer, i):
+        to_core(buffer, i).wait_recv()
+        ys[i] = (buffer[i].astype(F32) + cr[i].astype(F32)).astype(BF)
+        if i < 2:
+            for way in range(2):
+                y_half(way, i).start()
+
+    def y_second():
+        for way in range(2):
+            for side in range(2):
+                y_half(way, side).wait_recv()
+                add_rows(ys.at[2 + 2 * way + side, pl.ds(way * HB, HB), :], yh.at[way, side])
+                y_full(way, side).start()
+
+    def parts(buffer, part, sums, lo, hi):
+        for i in range(lo, hi):
             buffer[i] = term(feature(i), part).astype(BF)
 
-    def pass_core(buffer):
-        @pl.loop(0, NQ)
-        def _(i):
-            to_core(buffer, i).start()
-
-    def join(buffer):
-        def one(i):
-            to_core(buffer, i).wait_recv()
-            ys[i] = (buffer[i].astype(F32) + cr[i].astype(F32)).astype(BF)
-
-        @pl.loop(0, NQ - 2)
-        def _(i):
-            one(i)
-            to_y(i).start()
-
-        @pl.loop(NQ - 2, NQ)
-        def _(i):
-            one(i)
-
-    parts(po, 0)
-
-    @pl.when(jnp.logical_not(keeps))
-    def _():
-        pass_core(po)
+            @pl.when(sums)
+            def _(i=i):
+                if i > 0:
+                    join(buffer, i - 1)
+                if i == NQ - 1:
+                    join(buffer, i)
+
+            @pl.when(jnp.logical_not(sums))
+            def _(i=i):
+                to_core(buffer, i).start()
+
+    def y_sum(which):
+        total = ys[6 + which].astype(F32)
+        for way in range(2):
+            total = total + yr[way, which].astype(F32)
+        return total
+
+    swap = remote(xs, xv, xh_ss, xh_rs, tensor=((1 - xh) * NY + y) * 2 + core)
+
+    def y_third():
+        for way in range(2):
+            for side in range(2):
+                y_full(way, side).wait_recv()
+        xs[...] = y_sum(1 - xh).astype(BF)
+        swap.start()
+        ng[...] = y_sum(xh)
+
+    def x_last():
+        swap.wait_recv()
+        ng[...] = ng[...] + xv[...].astype(F32)
+
+    away = jnp.logical_not(keeps)
 
     def complete(j):
-        swap_grad(j).wait_recv()
+        if j != 1:
+            swap_grad(j).wait_recv()
 
         @pl.loop(0, NZ)
         def _(zs):
@@ -484,71 +545,73 @@
         if s == 5:
             gq[j] = con[z, j].astype(F32) * (1.0 / NR)
 
+    contribute(2)
+    turn(0, qg)
+    parts(po, 0, keeps, 0, NQ)
     complete(2)
     ring(2, 1)
+
+    @pl.when(keeps)
+    def _():
+        y_second()
+
+    contribute(0)
+    ring(2, 2)
+    complete(0)
+    ring(0, 1)
+    contribute(1)
+    swap_grad(1).wait_recv()
+    turn(1, qo)
+    parts(px, 1, away, 0, 4)
+    ring(2, 3)
+    ring(0, 2)
+    parts(px, 1, away, 4, NQ)
+    complete(1)
+    ring(1, 1)
+    ring(2, 4)
+
+    @pl.when(away)
+    def _():
+        y_second()
+
+    ring(0, 3)
     cp_part[...] = dot(attn[...], folded[...]).astype(BF)
     sum_t2 = Sum("tensor", cp_part, code, t2)
     sum_t2.first()
     mx_part[...] = dot_tn(attn[...], cg[...]).astype(BF)
     sum_d2 = Sum("dp", mx_part, mixing, d2)
     sum_d2.first()
-    ring(2, 2)
-    complete(0)
-    ring(0, 1)
 
     @pl.when(keeps)
     def _():
-        join(po)
-
-    ring(2, 3)
-    ring(0, 2)
-    complete(1)
-    ring(1, 1)
-    turn(1, qo)
-    parts(px, 1)
+        y_third()
+
+    ring(1, 2)
+    ring(2, 5)
+    ring(0, 4)
+    sum_t2.second()
+    sum_d2.second()
+
+    @pl.when(away)
+    def _():
+        y_third()
+
+    ring(1, 3)
+    sum_t2.third()
 
     @pl.when(keeps)
     def _():
-        pass_core(px)
-
-    ring(2, 4)
-    ring(0, 3)
-    ring(1, 2)
+        x_last()
+
+    ring(0, 5)
+    sum_d2.third()
+    ring(1, 4)
+    sum_t2.across()
+    home = remote(fs, fv, fs_ss, fs_rs, dp=other, tensor=sibling)
 
     @pl.when(jnp.logical_not(keeps))
     def _():
-        join(px)
-
-    sum_t2.second()
-    sum_d2.second()
-    ring(2, 5)
-    ring(0, 4)
-    ring(1, 3)
-    sum_t2.third()
-
-    for i in range(NQ - 2):
-        remote(yr.at[i], yr.at[i], y_ss.at[i], y_rs.at[i], tensor=tensor).wait_recv()
-
-    def y_sum(which):
-        total = ys[6 + which].astype(F32)
-        for k in range(3):
-            total = total + yr[2 * k + which].astype(F32)
-        return total
-
-    xs[...] = y_sum(1 - xh).astype(BF)
-    swap = remote(xs, xv, xh_ss, xh_rs, tensor=((1 - xh) * NY + y) * 2 + core)
-    swap.start()
-    ng[...] = y_sum(xh)
-    sum_d2.third()
-    ring(0, 5)
-    ring(1, 4)
-    sum_t2.across()
-    swap.wait_recv()
-    ng[...] = ng[...] + xv[...].astype(F32)
-    home = remote(fs, fv, fs_ss, fs_rs, dp=other, tensor=sibling)
-
-    @pl.when(jnp.logical_not(keeps))
-    def _():
+        x_last()
         fs[...] = ng[...].astype(BF)
         home.start()
         home.wait_recv()
@@ -606,9 +669,10 @@
     def _(i):
         to_core(po, i).wait_send()
 
-    @pl.loop(0, NQ - 2)
-    def _(i):
-        to_y(i).wait_send()
+    for way in range(2):
+        for side in range(2):
+            y_half(way, side).wait_send()
+            y_full(way, side).wait_send()
 
 
 def sublayer(*args):
@@ -628,12 +692,12 @@
         v(BF, SEQ, W3), v(BF, SEQ, 256), v(BF, SEQ, 256), v(BF, SEQ, W3), v(BF, SEQ, W3), v(BF, 2, W3, SEQ),
         v(F32, SEQ, 512),
         v(BF, NZ, 3, BLK, 256), v(BF, 3, 2, HB, 256), v(BF, 3, 2, 3, BLK, 256),
-        v(BF, NQ, BLK, SEQ), v(BF, NQ, BLK, SEQ), v(BF, NQ, BLK, SEQ), v(BF, NQ, BLK, SEQ), v(BF, NQ - 2, BLK, SEQ),
+        v(BF, NQ, BLK, SEQ), v(BF, NQ, BLK, SEQ), v(BF, NQ, BLK, SEQ), v(BF, NQ, BLK, SEQ), v(BF, 2, 2, HB, SEQ), v(BF, 2, 2, BLK, SEQ),
         v(BF, BLK, SEQ), v(BF, BLK, SEQ), v(BF, BLK, SEQ), v(BF, BLK, SEQ), v(F32, BLK, SEQ),
         v(F32, NR, 8, SEQ), v(F32, NR, 8, 384), v(BF, SEQ, C), v(BF, 256, C), v(BF, SEQ, C), v(BF, 256, C),
         sum_buffers(SEQ, NY), sum_buffers(256, NZ), sum_buffers(SEQ, NY), sum_buffers(256, NZ),
         dma(4), one, dma(2, 3, 4), dma(2, 3, 4), dma(4, 4), dma(4, 4), dma(4, 4), dma(4, 4), dma(3), dma(3), dma(3), dma(3),
-        dma(3, 2), dma(3, 2), dma(3, 2, 3), dma(3, 2, 3), dma(NQ), dma(NQ), dma(NQ), dma(NQ), one, one, one, one,
+        dma(3, 2), dma(3, 2), dma(3, 2, 3), dma(3, 2, 3), dma(NQ), dma(NQ), dma(2, 2), dma(2, 2), dma(2, 2), dma(2, 2), one, one, one, one,
         dma(NR), dma(NR), dma(NR), dma(NR),
     ]
     return pl.pallas_call(
@@ -652,6 +716,28 @@
             collective_id=0, has_side_effects=True, vmem_limit_bytes=62 * 2**20
         ),
     )(*args)
+
+
+def place_kernel(*refs):
+    n = len(refs) // 2
+    *refs, sems = refs
+    copies = [pltpu.make_async_copy(refs[i], refs[n + i], sems.at[i]) for i in range(n)]
+    for copy in copies:
+        copy.start()
+    for copy in copies:
+        copy.wait()
+
+
+def place(*arrays):
+    far = pl.BlockSpec(memory_space=pl.ANY)
+    return pl.pallas_call(
+        place_kernel,
+        out_shape=[jax.ShapeDtypeStruct(a.shape, a.dtype) for a in arrays],
+        in_specs=[far] * len(arrays),
+        out_specs=[far] * len(arrays),
+        scratch_shapes=[dma(len(arrays))],
+        compiler_params=pltpu.CompilerParams(vmem_limit_bytes=62 * 2**20),
+    )(*arrays)
 
 
 def local(
@@ -674,6 +760,9 @@
         decoder.T,
         grad_output.T,
     )
+    residual_out, grad_input, grad_qkv, grad_out_weight = place(
+        residual_out, grad_input, grad_qkv, grad_out_weight
+    )
     return residual_out.T, grad_input.T, grad_qkv, grad_out_weight.T, sums[0, :BLK], sums[1, :BLK]
 
 

time: 174 us -> 228 us (1.31); the launches traced: 174 us -> 225 us
  Pallas kernels: 164 us -> 223 us
  local copies, waits for them, and re-layouts: 8.74 us -> 1.38 us
    pallas_call x0 -> x1, Pallas kernels: none -> 60.7 us  [place(): pl.pallas_call(place_kernel, out_shape=[jax.ShapeDtypeStruct(a.shape, a.d...]
    unnamed x4 -> x0, local copies, waits for them, and re-layouts: 7.36 us -> none
where the time goes in v4:
time: 228 us; the launch traced here: 225 us
  Pallas kernels  223 us (98%)
    pallas_call x1, Pallas kernels, sublayer(): pl.pallas_call(kernel, out_shape=[shape((BLK, SEQ), BF), shape((BLK, SEQ)...  162 us
    pallas_call x1, Pallas kernels, place(): pl.pallas_call(place_kernel, out_shape=[jax.ShapeDtypeStruct(a.shape, a.d...  60.7 us

profile of v4, /device:TPU:1, one launch (start us, length us, event | category | flops | bytes accessed | tf_op | source)
XLA Modules:
  0.0 225.0 jit_solution(8925557818611923147)
XLA Ops:
  0.6 162.2 %shard_map.127 = (bf16[320,512]{1,0:T(8,128)(2,1)}, bf16[320,512]{1,0:T(8,128)(2,1)}, f32[3,320,256]{2,1,0:T(8,128)}, f32[320,256]{1,0:T(8,128)}, f32[8,384]{1,0:T(8,128)}) custom-call(bf16[512,5120]{1,0:T(8,128)(2,1)} %x_hbm.1, f32[1,5120]{1,0:T(1,128)} %bitcast.11, f32[1,5120]{1,0:T(1,128)} %bitcast.12, bf16[3,320,256]{2,1,0:T(8,128)(2,1)} %w_in.1, ...), custom_call_target="tpu_custom_call" | custom-call | tf_op jit(solution)/shard_map/pallas_call | solution.py:703
  162.9 60.7 %shard_map.128 = (bf16[320,512]{1,0:T(8,128)(2,1)}, bf16[320,512]{1,0:T(8,128)(2,1)}, f32[3,320,256]{2,1,0:T(8,128)}, f32[320,256]{1,0:T(8,128)}) custom-call(bf16[320,512]{1,0:T(8,128)(2,1)} %get-tuple-element.15.refs_0_, bf16[320,512]{1,0:T(8,128)(2,1)} %get-tuple-element.16.refs_1_, f32[3,320,256]{2,1,0:T(8,128)} %get-tuple-element.17.refs_2_, ...), custom_call_target="tpu_custom_call" | custom-call | tf_op jit(solution)/shard_map/pallas_call | solution.py:733
  223.6 1.4 slice_reduce_fusion

commit v5 on v4

--- a/solution.py
+++ b/solution.py
@@ -166,7 +166,7 @@
     x_hbm, gain, bias, w_in, owt, enc, dect, got,
     ro_t, gi_t, gq, gow_t, gb,
     x, w, nb, no, acc, mu, rstd, xt, gcol, hat, st,
-    cg_part, fo_part, cg, folded, ps, pr, qkvt, qkv, ag, attn, qg, qo, qgt, dkv,
+    cg_part, fo_part, cg, folded, ps, pr, qkvt, qkv, ag, attn, qg, qo, qgt, dkv, pp,
     con, rb1, rb, po, px, cr, ys, yh, yr, xs, xv, fs, fv, ng, lt, gs, cp_part, mx_part, code, mixing,
     t1, d1, t2, d2,
     x_sem, loc, a_ss, a_rs, n_ss, n_rs, f_ss, f_rs, p_ss, p_rs, q_ss, q_rs,
@@ -335,6 +335,13 @@
         use_all(j, 0, 8, 1)
         give(j)
 
+    def far_begin():
+        use_all(2, 0, 7, 1)
+
+    def far_end():
+        use_all(2, 7, 8, 1)
+        give(2)
+
     add(1.2, start_folded)
     for r in range(4):
         add(1.3, norm, r, 0, 4)
@@ -347,13 +354,13 @@
     events = [
         (5.0, relay_use, 0, 1),
         (7.0, sum_d.second),
-        (8.3, relay_use, 1, 1),
-        (11.6, relay_use, 0, 2),
+        (8.5, relay_use, 1, 1),
+        (12.0, relay_use, 0, 2),
         (13.5, forward_on, 0),
-        (16.5, relay_use, 1, 2),
-        (16.6, send_own, 2),
-        (19.0, sum_d.third),
-        (20.0, relay_use, 0, 3),
+        (15.5, relay_use, 1, 2),
+        (15.6, send_own, 2),
+        (19.0, relay_use, 0, 3),
+        (19.5, sum_d.third),
         (20.5, forward_on, 1),
         (21.0, own_use),
         (21.5, sum_t.second),
@@ -361,19 +368,20 @@
         (25.5, sum_t.third),
         (28.0, relay_use, 1, 3),
         (28.0, forward_on, 2),
-        (29.5, sum_t.across),
-        (31.0, relay_use, 0, 4),
-        (31.5, sum_d.fourth),
-        (34.0, relay_use, 2, 2),
-        (34.2, sum_t.fourth),
+        (30.0, relay_use, 0, 4),
+        (31.0, sum_d.fourth),
+        (32.0, sum_t.across),
+        (33.0, relay_use, 2, 2),
         (35.0, forward_on, 3),
         (36.0, relay_use, 1, 4),
         (37.5, collect),
         (38.0, far_use, 0),
-        (39.5, relay_use, 2, 3),
-        (40.0, far_use, 1),
+        (39.0, relay_use, 2, 3),
+        (39.5, far_use, 1),
+        (42.0, far_begin),
         (43.0, relay_use, 2, 4),
-        (43.0, far_use, 2),
+        (43.0, far_end),
+        (44.0, sum_t.fourth),
     ]
     now = 0.0
     for when, f, *args in events:
@@ -382,52 +390,62 @@
             g()
             now += cost
         f(*args)
-        now = max(now, when) + (2.8 if f is far_use else 0.2)
+        now = max(now, when) + (2.5 if f in (far_use, far_begin) else 0.2)
     while work:
         work.popleft()[1]()
-    sum_d.last()
-    sum_t.last()
-    ag[...] = dot_nt(cg[...], folded[...]).astype(BF)
     mine_rows = rows(core * BLK, BLK)
     rs_row = rstd[...].T[0:1, :]
     hat[...] = (xt[mine_rows, :].astype(F32) - mu[...].T[0:1, :]) * rs_row
     st[0:1, :] = rs_row
     gcol[...] = jnp.broadcast_to(gain[0:1, slab_cols(q)], (128, SLAB)).T
     dkv[...] = jnp.zeros_like(dkv)
-    for j in range(3):
-        take(j)
+    take(0)
+    take(1)
 
     rate = HDIM**-0.5
-    for h in range(2):
-        cq = slice(h * HDIM, (h + 1) * HDIM)
-        ck = slice(256 + h * HDIM, 256 + (h + 1) * HDIM)
-        cv = slice(512 + h * HDIM, 512 + (h + 1) * HDIM)
-        for r in range(4):
-            here, n = slice(r * 128, (r + 1) * 128), 128 * (r + 1)
-            qb, kb, vb = qkv[here, cq], qkv[0:n, ck], qkv[0:n, cv]
-            s = dot_nt(qb, kb) * rate
-            at_row = lax.broadcasted_iota(jnp.int32, (128, n), 0) + r * 128
-            at_col = lax.broadcasted_iota(jnp.int32, (128, n), 1)
-            s = jnp.where(at_col <= at_row, s, -1e30)
-            e = jnp.exp(s - jnp.max(s, axis=1, keepdims=True))
-            p = e * (1.0 / jnp.sum(e, axis=1, keepdims=True))
-            pb = p.astype(BF)
-            attn[here, cq] = dot(pb, vb).astype(BF)
-            da = ag[here, cq]
-            dpr = dot_nt(da, vb).astype(BF).astype(F32)
-            ds = p * (dpr - jnp.sum(p * dpr, axis=1, keepdims=True))
-            ds = (ds * rate).astype(BF)
-            qg[here, cq] = dot(ds, kb).astype(BF)
-            dkv[0:n, cq] += dot_tn(ds, qb)
-            dkv[0:n, ck] += dot_tn(pb, da)
-    qg[:, 256:768] = dkv[...].astype(BF)
+    blocks = [(h, r) for h in range(2) for r in range(4)]
+
+    def cut(h, r):
+        return slice(h * HDIM, (h + 1) * HDIM), slice(r * 128, (r + 1) * 128), 128 * (r + 1)
+
+    def columns(j, h):
+        return slice(j * 256 + h * HDIM, j * 256 + (h + 1) * HDIM)
+
+    for h, r in blocks:
+        _, here, n = cut(h, r)
+        s = dot_nt(qkv[here, columns(0, h)], qkv[0:n, columns(1, h)]) * rate
+        at_row = lax.broadcasted_iota(jnp.int32, (128, n), 0) + r * 128
+        at_col = lax.broadcasted_iota(jnp.int32, (128, n), 1)
+        s = jnp.where(at_col <= at_row, s, -1e30)
+        e = jnp.exp(s - jnp.max(s, axis=1, keepdims=True))
+        pp[h, here, 0:n] = e * (1.0 / jnp.sum(e, axis=1, keepdims=True))
+    sum_t.last()
+    sum_d.last()
+    ag[...] = dot_nt(cg[...], folded[...]).astype(BF)
+    take(2)
+    for h, r in blocks:
+        cq, here, n = cut(h, r)
+        pb = pp[h, here, 0:n].astype(BF)
+        attn[here, cq] = dot(pb, qkv[0:n, columns(2, h)]).astype(BF)
+        dkv[0:n, columns(1, h)] += dot_tn(pb, ag[here, cq])
+    qg[:, 512:768] = dkv[:, 256:512].astype(BF)
 
     def swap_grad(j):
         here = pl.ds(j * 256, 256)
         return remote(qg.at[:, here], qo.at[:, here], q_ss.at[j], q_rs.at[j], dp=other)
 
-    for j in (2, 0, 1):
-        go(swap_grad(j))
+    go(swap_grad(2))
+    for h, r in blocks:
+        cq, here, n = cut(h, r)
+        p, vb = pp[h, here, 0:n], qkv[0:n, columns(2, h)]
+        dpr = dot_nt(ag[here, cq], vb).astype(BF).astype(F32)
+        ds = p * (dpr - jnp.sum(p * dpr, axis=1, keepdims=True))
+        ds = (ds * rate).astype(BF)
+        qg[here, cq] = dot(ds, qkv[0:n, columns(1, h)]).astype(BF)
+        dkv[0:n, cq] += dot_tn(ds, qkv[here, columns(0, h)])
+    go(swap_grad(0))
+    qg[:, 256:512] = dkv[:, 0:256].astype(BF)
+    go(swap_grad(1))
 
     def contribute(j):
         @pl.loop(0, NZ)
@@ -546,74 +564,79 @@
             gq[j] = con[z, j].astype(F32) * (1.0 / NR)
 
     contribute(2)
+    cp_part[...] = dot(attn[...], folded[...]).astype(BF)
+    sum_t2 = Sum("tensor", cp_part, code, t2)
+    sum_t2.first()
     turn(0, qg)
-    parts(po, 0, keeps, 0, NQ)
     complete(2)
     ring(2, 1)
+    mx_part[...] = dot_tn(attn[...], cg[...]).astype(BF)
+    sum_d2 = Sum("dp", mx_part, mixing, d2)
+    sum_d2.first()
+    parts(po, 0, keeps, 0, 4)
+    sum_t2.second()
+    ring(2, 2)
+    parts(po, 0, keeps, 4, NQ)
+    contribute(0)
+    complete(0)
+    ring(0, 1)
+    ring(2, 3)
+    sum_t2.third()
 
     @pl.when(keeps)
     def _():
         y_second()
 
-    contribute(0)
-    ring(2, 2)
-    complete(0)
-    ring(0, 1)
     contribute(1)
+    ring(0, 2)
     swap_grad(1).wait_recv()
     turn(1, qo)
     parts(px, 1, away, 0, 4)
-    ring(2, 3)
-    ring(0, 2)
+    ring(2, 4)
+    sum_t2.across()
     parts(px, 1, away, 4, NQ)
+    ring(0, 3)
     complete(1)
     ring(1, 1)
-    ring(2, 4)
+
+    @pl.when(keeps)
+    def _():
+        y_third()
 
     @pl.when(away)
     def _():
         y_second()
 
-    ring(0, 3)
-    cp_part[...] = dot(attn[...], folded[...]).astype(BF)
-    sum_t2 = Sum("tensor", cp_part, code, t2)
-    sum_t2.first()
-    mx_part[...] = dot_tn(attn[...], cg[...]).astype(BF)
-    sum_d2 = Sum("dp", mx_part, mixing, d2)
-    sum_d2.first()
+    sum_d2.second()
+    ring(2, 5)
+    ring(1, 2)
+    ring(0, 4)
+    sum_t2.fourth()
 
     @pl.when(keeps)
     def _():
-        y_third()
-
-    ring(1, 2)
-    ring(2, 5)
-    ring(0, 4)
-    sum_t2.second()
-    sum_d2.second()
+        x_last()
 
     @pl.when(away)
     def _():
         y_third()
 
     ring(1, 3)
-    sum_t2.third()
-
-    @pl.when(keeps)
-    def _():
-        x_last()
-
+    sum_d2.third()
     ring(0, 5)
-    sum_d2.third()
-    ring(1, 4)
-    sum_t2.across()
     home = remote(fs, fv, fs_ss, fs_rs, dp=other, tensor=sibling)
 
-    @pl.when(jnp.logical_not(keeps))
+    @pl.when(away)
     def _():
         x_last()
         fs[...] = ng[...].astype(BF)
         home.start()
+
+    ring(1, 4)
+    sum_d2.fourth()
+
+    @pl.when(away)
+    def _():
         home.wait_recv()
         ng[...] = fv[...].astype(F32)
 
@@ -635,9 +658,6 @@
     slot = gs.at[dp]
     for k in range(1, NR):
         go(remote(slot, slot, gs_ss.at[k], gs_rs.at[k], dp=rem(dp + k, NR)))
-    sum_d2.fourth()
-    sum_t2.fourth()
-    ring(1, 5)
     sum_t2.last()
     ro_t[...] = (xt[mine_rows, :].astype(F32) + dot_nt(dect[...], code[...])).astype(BF)
 
@@ -648,6 +668,7 @@
     lead, trail = sums[0:1, :] * (1.0 / D), sums[1:2, :] * (1.0 / D)
     scaled = ng[...] * gcol[mine_rows, 0:1]
     gi_t[...] = (got[...].astype(F32) + st[0:1, :] * (scaled - lead - hat[...] * trail)).astype(BF)
+    ring(1, 5)
     sum_d2.last()
     gow_t[...] = dot_nt(enc[...], mixing[...]) * (1.0 / NR)
     for k in range(1, NR):
@@ -690,7 +711,7 @@
         v(F32, SEQ, 128), v(F32, SEQ, 128), v(BF, SLAB, SEQ), v(F32, SLAB, 128), v(F32, BLK, SEQ), v(F32, 8, SEQ),
         v(BF, SEQ, C), v(BF, 256, C), v(BF, SEQ, C), v(BF, 256, C), v(BF, W3, SEQ), v(BF, W3, SEQ), v(BF, W3, SEQ),
         v(BF, SEQ, W3), v(BF, SEQ, 256), v(BF, SEQ, 256), v(BF, SEQ, W3), v(BF, SEQ, W3), v(BF, 2, W3, SEQ),
-        v(F32, SEQ, 512),
+        v(F32, SEQ, 512), v(F32, 2, SEQ, SEQ),
         v(BF, NZ, 3, BLK, 256), v(BF, 3, 2, HB, 256), v(BF, 3, 2, 3, BLK, 256),
         v(BF, NQ, BLK, SEQ), v(BF, NQ, BLK, SEQ), v(BF, NQ, BLK, SEQ), v(BF, NQ, BLK, SEQ), v(BF, 2, 2, HB, SEQ), v(BF, 2, 2, BLK, SEQ),
         v(BF, BLK, SEQ), v(BF, BLK, SEQ), v(BF, BLK, SEQ), v(BF, BLK, SEQ), v(F32, BLK, SEQ),
@@ -733,10 +754,9 @@
     return pl.pallas_call(
         place_kernel,
         out_shape=[jax.ShapeDtypeStruct(a.shape, a.dtype) for a in arrays],
-        in_specs=[far] * len(arrays),
+        in_specs=[pl.BlockSpec(memory_space=pltpu.VMEM)] * len(arrays),
         out_specs=[far] * len(arrays),
         scratch_shapes=[dma(len(arrays))],
-        compiler_params=pltpu.CompilerParams(vmem_limit_bytes=62 * 2**20),
     )(*arrays)
 
 

time: 228 us -> 156 us (0.68); the launches traced: 225 us -> 155 us
  Pallas kernels: 223 us -> 153 us
    pallas_call x1, Pallas kernels: 60.7 us -> 2.77 us  [place(): pl.pallas_call(place_kernel, out_shape=[jax.ShapeDtypeStruct(a.shape, a.d...]
    pallas_call x1, Pallas kernels: 162 us -> 151 us  [sublayer(): pl.pallas_call(kernel, out_shape=[shape((BLK, SEQ), BF), shape((BLK, SEQ)...]
where the time goes in v5:
time: 156 us; the launch traced here: 155 us
  Pallas kernels  153 us (98%)
    pallas_call x1, Pallas kernels, sublayer(): pl.pallas_call(kernel, out_shape=[shape((BLK, SEQ), BF), shape((BLK, SEQ)...  151 us

profile of v5, /device:TPU:1, one launch (start us, length us, event | category | flops | bytes accessed | tf_op | source)
XLA Modules:
  0.0 155.3 jit_solution(95259451430663191)
XLA Ops:
  0.6 150.5 %shard_map.127 = (bf16[320,512]{1,0:T(8,128)(2,1)}, bf16[320,512]{1,0:T(8,128)(2,1)}, f32[3,320,256]{2,1,0:T(8,128)}, f32[320,256]{1,0:T(8,128)}, f32[8,384]{1,0:T(8,128)}) custom-call(bf16[512,5120]{1,0:T(8,128)(2,1)} %x_hbm.1, f32[1,5120]{1,0:T(1,128)} %bitcast.11, f32[1,5120]{1,0:T(1,128)} %bitcast.12, bf16[3,320,256]{2,1,0:T(8,128)(2,1)} %w_in.1, ...), custom_call_target="tpu_custom_call" | custom-call | tf_op jit(solution)/shard_map/pallas_call | solution.py:724
  151.2 2.8 %shard_map.128 = (bf16[320,512]{1,0:T(8,128)(2,1)}, bf16[320,512]{1,0:T(8,128)(2,1)}, f32[3,320,256]{2,1,0:T(8,128)}, f32[320,256]{1,0:T(8,128)}) custom-call(bf16[320,512]{1,0:T(8,128)(2,1)} %get-tuple-element.15.refs_0_, bf16[320,512]{1,0:T(8,128)(2,1)} %get-tuple-element.16.refs_1_, f32[3,320,256]{2,1,0:T(8,128)} %get-tuple-element.17.refs_2_, ...), custom_call_target="tpu_custom_call" | custom-call | tf_op jit(solution)/shard_map/pallas_call | solution.py:754
  153.9 1.4 slice_reduce_fusion

commit v6 on v5

--- a/solution.py
+++ b/solution.py
@@ -53,9 +53,11 @@
         for k in range(1, NR):
             pl.semaphore_signal(barrier, inc=1, device_id={axis: rem(me + k, NR)}, device_id_type=MESH)
     dp, tensor = lax.axis_index("dp"), lax.axis_index("tensor")
-    across = {"dp": dp + 1 - 2 * rem(dp, 2), "tensor": tensor + 1 - 2 * rem(tensor, 2)}
-    pl.semaphore_signal(barrier, inc=1, device_id=across, device_id_type=MESH)
-    pl.semaphore_wait(barrier, 2 * (NR - 1) + 1)
+    flip = tensor + 1 - 2 * rem(tensor, 2)
+    for there in (flip, rem(flip + 8, NR)):
+        across = {"dp": dp + 1 - 2 * rem(dp, 2), "tensor": there}
+        pl.semaphore_signal(barrier, inc=1, device_id=across, device_id_type=MESH)
+    pl.semaphore_wait(barrier, 2 * NR)
 
 
 class Sum:
@@ -166,10 +168,10 @@
     x_hbm, gain, bias, w_in, owt, enc, dect, got,
     ro_t, gi_t, gq, gow_t, gb,
     x, w, nb, no, acc, mu, rstd, xt, gcol, hat, st,
-    cg_part, fo_part, cg, folded, ps, pr, qkvt, qkv, ag, attn, qg, qo, qgt, dkv, pp,
-    con, rb1, rb, po, px, cr, ys, yh, yr, xs, xv, fs, fv, ng, lt, gs, cp_part, mx_part, code, mixing,
+    cg_part, fo_part, cg, folded, ps, pr, qkv, ag, attn, qg, qo, qgt, dkv,
+    con, rb1, rb, po, px, cr, ys, yh, yr, fs, fv, ng, lt, gs, code, mixing,
     t1, d1, t2, d2,
-    x_sem, loc, a_ss, a_rs, n_ss, n_rs, f_ss, f_rs, p_ss, p_rs, q_ss, q_rs,
+    x_sem, loc, a_ss, a_rs, n_ss, n_rs, g_ss, g_rs, f_ss, f_rs, p_ss, p_rs, q_ss, q_rs,
     r1_ss, r1_rs, r_ss, r_rs, cs_ss, cs_rs, yh_ss, yh_rs, y_ss, y_rs, xh_ss, xh_rs, fs_ss, fs_rs, lt_ss, lt_rs, gs_ss, gs_rs,
 ):
     dp, tensor = lax.axis_index("dp"), lax.axis_index("tensor")
@@ -240,13 +242,20 @@
     def tokens(r):
         return pl.ds(r * 128, 128)
 
-    def cross(k, r):
-        zs = near(2 * k + core)
-        src, dst = nb.at[1, zs, :, tokens(r)], no.at[zs, :, tokens(r)]
-        return remote(src, dst, n_ss.at[k, r], n_rs.at[k, r], dp=other)
+    def piece(k, c, r):
+        return no.at[near(2 * k + c), :, tokens(r)]
+
+    def cross(r):
+        src = nb.at[1, near(2 * y + core), :, tokens(r)]
+        return remote(src, piece(y, core, r), n_ss.at[r], n_rs.at[r], dp=other)
+
+    def along(k, r):
+        part = piece(y, core, r)
+        there = (xh * NY + rem(y + k, NY)) * 2 + core
+        return remote(part, part, g_ss.at[k - 1, r], g_rs.at[k - 1, r], tensor=there)
 
     def pass_on(k, r):
-        part = no.at[near(2 * k + core), :, tokens(r)]
+        part = piece(rem(y + NY - k, NY), core, r)
         return remote(part, part, f_ss.at[k, r], f_rs.at[k, r], tensor=sibling)
 
     def norm(r, lo, hi):
@@ -273,12 +282,18 @@
             nb[xl, zs, :, r * 128 : (r + 1) * 128] = v[0:BLK]
             nb[1 - xl, zs, :, r * 128 : (r + 1) * 128] = v[BLK:SLAB]
 
-        for k in range(4):
-            go(cross(k, r))
+        go(cross(r))
 
     def forward_on(r):
-        for k in range(4):
-            cross(k, r).wait_recv()
+        cross(r).wait_recv()
+        for k in (2, 1, 3):
+            go(along(k, r))
+        go(pass_on(0, r))
+
+    def share(r):
+        for k in (1, 3, 2):
+            part = piece(rem(y + NY - k, NY), core, r)
+            remote(part, part, g_ss.at[k - 1, r], g_rs.at[k - 1, r], tensor=sibling).wait_recv()
             go(pass_on(k, r))
 
     def use(j, i, part):
@@ -304,19 +319,27 @@
     def take(j):
         here = slice(j * 256, (j + 1) * 256)
         partial(j).wait_recv()
-        qkvt[here, :] = (acc[0, here, :] + pr[here, :].astype(F32)).astype(BF)
-        qkv[:, here] = qkvt[here, :].T
+        qkv[:, here] = (acc[0, here, :] + pr[here, :].astype(F32)).astype(BF).T
 
     def collect():
         for r in range(4):
             for k in range(4):
-                part = no.at[near(2 * k + 1 - core), :, tokens(r)]
+                part = piece(rem(y + NY - k, NY), 1 - core, r)
                 remote(part, part, f_ss.at[k, r], f_rs.at[k, r], tensor=sibling).wait_recv()
 
     work = deque()
 
     def add(cost, f, *args):
-        work.append((cost, functools.partial(f, *args)))
+        work.append((cost, f, args))
+
+    def run():
+        cost, f, args = work.popleft()
+        f(*args)
+        return cost
+
+    def ahead(f, *args):
+        while any(piece[1:] == (f, args) for piece in work):
+            run()
 
     def clear():
         acc[...] = jnp.zeros_like(acc)
@@ -354,50 +377,60 @@
     events = [
         (5.0, relay_use, 0, 1),
         (7.0, sum_d.second),
+        (8.3, forward_on, 0),
         (8.5, relay_use, 1, 1),
         (12.0, relay_use, 0, 2),
-        (13.5, forward_on, 0),
+        (13.0, forward_on, 1),
+        (13.2, share, 0),
         (15.5, relay_use, 1, 2),
         (15.6, send_own, 2),
+        (17.0, forward_on, 2),
+        (17.2, share, 1),
         (19.0, relay_use, 0, 3),
         (19.5, sum_d.third),
-        (20.5, forward_on, 1),
+        (20.5, forward_on, 3),
         (21.0, own_use),
+        (21.5, share, 2),
         (21.5, sum_t.second),
         (24.0, relay_use, 2, 1),
+        (25.0, share, 3),
         (25.5, sum_t.third),
-        (28.0, relay_use, 1, 3),
-        (28.0, forward_on, 2),
-        (30.0, relay_use, 0, 4),
+        (27.0, relay_use, 1, 3),
+        (27.5, collect),
+        (29.0, relay_use, 0, 4),
+        (29.5, far_use, 0),
         (31.0, sum_d.fourth),
-        (32.0, sum_t.across),
+        (31.5, sum_t.across),
         (33.0, relay_use, 2, 2),
-        (35.0, forward_on, 3),
-        (36.0, relay_use, 1, 4),
-        (37.5, collect),
-        (38.0, far_use, 0),
+        (35.0, relay_use, 1, 4),
+        (35.5, far_use, 1),
+        (38.5, sum_t.fourth),
         (39.0, relay_use, 2, 3),
-        (39.5, far_use, 1),
-        (42.0, far_begin),
+        (39.5, far_begin),
+        (42.5, sum_t.last),
         (43.0, relay_use, 2, 4),
         (43.0, far_end),
-        (44.0, sum_t.fourth),
     ]
     now = 0.0
     for when, f, *args in events:
         while work and now + work[0][0] <= when + 0.3:
-            cost, g = work.popleft()
-            g()
-            now += cost
+            now += run()
+        if f is forward_on:
+            ahead(spread, *args)
+        elif f == sum_d.second:
+            ahead(start_folded)
+        elif f == sum_t.second:
+            ahead(start_code_grad)
         f(*args)
         now = max(now, when) + (2.5 if f in (far_use, far_begin) else 0.2)
     while work:
-        work.popleft()[1]()
+        run()
     mine_rows = rows(core * BLK, BLK)
     rs_row = rstd[...].T[0:1, :]
     hat[...] = (xt[mine_rows, :].astype(F32) - mu[...].T[0:1, :]) * rs_row
     st[0:1, :] = rs_row
-    gcol[...] = jnp.broadcast_to(gain[0:1, slab_cols(q)], (128, SLAB)).T
+    turned = jnp.broadcast_to(gain[0:1, slab_cols(q)], (128, SLAB)).T
+    gcol[...] = jnp.where(core == 0, turned[0:BLK], turned[BLK:SLAB])
     dkv[...] = jnp.zeros_like(dkv)
     take(0)
     take(1)
@@ -418,26 +451,31 @@
         at_col = lax.broadcasted_iota(jnp.int32, (128, n), 1)
         s = jnp.where(at_col <= at_row, s, -1e30)
         e = jnp.exp(s - jnp.max(s, axis=1, keepdims=True))
-        pp[h, here, 0:n] = e * (1.0 / jnp.sum(e, axis=1, keepdims=True))
-    sum_t.last()
+        acc[h, here, 0:n] = e * (1.0 / jnp.sum(e, axis=1, keepdims=True))
     sum_d.last()
     ag[...] = dot_nt(cg[...], folded[...]).astype(BF)
+    for h, r in blocks:
+        cq, here, n = cut(h, r)
+        dkv[0:n, columns(1, h)] += dot_tn(acc[h, here, 0:n].astype(BF), ag[here, cq])
+    qg[:, 512:768] = dkv[:, 256:512].astype(BF)
+
+    def swap_grad(j):
+        here = pl.ds(j * 256, 256)
+        return remote(qg.at[:, here], qo.at[:, here], q_ss.at[j], q_rs.at[j], dp=other)
+
+    go(swap_grad(2))
+
+    def contribute(j):
+        @pl.loop(0, NZ)
+        def _(zs):
+            con[zs, j] = dot(nb[0, zs], qg[:, j * 256 : (j + 1) * 256]).astype(BF)
+
+    contribute(2)
     take(2)
     for h, r in blocks:
         cq, here, n = cut(h, r)
-        pb = pp[h, here, 0:n].astype(BF)
-        attn[here, cq] = dot(pb, qkv[0:n, columns(2, h)]).astype(BF)
-        dkv[0:n, columns(1, h)] += dot_tn(pb, ag[here, cq])
-    qg[:, 512:768] = dkv[:, 256:512].astype(BF)
-
-    def swap_grad(j):
-        here = pl.ds(j * 256, 256)
-        return remote(qg.at[:, here], qo.at[:, here], q_ss.at[j], q_rs.at[j], dp=other)
-
-    go(swap_grad(2))
-    for h, r in blocks:
-        cq, here, n = cut(h, r)
-        p, vb = pp[h, here, 0:n], qkv[0:n, columns(2, h)]
+        p, vb = acc[h, here, 0:n], qkv[0:n, columns(2, h)]
+        attn[here, cq] = dot(p.astype(BF), vb).astype(BF)
         dpr = dot_nt(ag[here, cq], vb).astype(BF).astype(F32)
         ds = p * (dpr - jnp.sum(p * dpr, axis=1, keepdims=True))
         ds = (ds * rate).astype(BF)
@@ -447,11 +485,6 @@
     qg[:, 256:512] = dkv[:, 0:256].astype(BF)
     go(swap_grad(1))
 
-    def contribute(j):
-        @pl.loop(0, NZ)
-        def _(zs):
-            con[zs, j] = dot(nb[0, zs], qg[:, j * 256 : (j + 1) * 256]).astype(BF)
-
     def turn(part, source):
         @pl.loop(0, 6)
         def _(i):
@@ -518,35 +551,54 @@
             total = total + yr[way, which].astype(F32)
         return total
 
-    swap = remote(xs, xv, xh_ss, xh_rs, tensor=((1 - xh) * NY + y) * 2 + core)
+    swap = remote(fs.at[0], fv.at[0], xh_ss, xh_rs, tensor=((1 - xh) * NY + y) * 2 + core)
 
     def y_third():
         for way in range(2):
             for side in range(2):
                 y_full(way, side).wait_recv()
-        xs[...] = y_sum(1 - xh).astype(BF)
+        fs[0] = y_sum(1 - xh).astype(BF)
         swap.start()
         ng[...] = y_sum(xh)
 
+    def home(which):
+        there = (xh * (1 - which) + (1 - xh) * which) * NY + y
+        return remote(
+            fs.at[which], fv.at[which], fs_ss.at[which], fs_rs.at[which], dp=other, tensor=there * 2 + 1 - core
+        )
+
+    def y_home():
+        for way in range(2):
+            for side in range(2):
+                y_full(way, side).wait_recv()
+        for which in range(2):
+            fs[which] = y_sum(xh * (1 - which) + (1 - xh) * which).astype(BF)
+            home(which).start()
+
     def x_last():
         swap.wait_recv()
-        ng[...] = ng[...] + xv[...].astype(F32)
+        ng[...] = ng[...] + fv[0].astype(F32)
 
     away = jnp.logical_not(keeps)
 
-    def complete(j):
-        if j != 1:
-            swap_grad(j).wait_recv()
-
-        @pl.loop(0, NZ)
-        def _(zs):
+    z4 = rem(z + 4, NZ)
+
+    def complete(j, lo, hi):
+        @pl.loop(lo, hi)
+        def _(i):
+            zs = rem(z4 + i, NZ)
             here = slice(j * 256, (j + 1) * 256)
             con[zs, j] = (con[zs, j].astype(F32) + dot(no[zs], qo[:, here])).astype(BF)
+
+    def open_ring(j):
+        swap_grad(j).wait_recv()
+        complete(j, 0, 1)
+        ring(j, 1)
 
     def ring(j, s):
         for way, to in ways:
             if s == 1:
-                half = con.at[rem(z + 4, NZ), j, pl.ds(way * HB, HB), :]
+                half = con.at[z4, j, pl.ds(way * HB, HB), :]
                 go(remote(half, rb1.at[j, way], r1_ss.at[j, way], r1_rs.at[j, way], dp=to))
                 continue
             zs = rem(z + (5 - s if way == 0 else NZ + s - 5), NZ)
@@ -563,85 +615,77 @@
         if s == 5:
             gq[j] = con[z, j].astype(F32) * (1.0 / NR)
 
-    contribute(2)
-    cp_part[...] = dot(attn[...], folded[...]).astype(BF)
-    sum_t2 = Sum("tensor", cp_part, code, t2)
+    sum_t.drain()
+    cg_part[...] = dot(attn[...], folded[...]).astype(BF)
+    sum_t2 = Sum("tensor", cg_part, code, t2)
     sum_t2.first()
     turn(0, qg)
-    complete(2)
-    ring(2, 1)
-    mx_part[...] = dot_tn(attn[...], cg[...]).astype(BF)
-    sum_d2 = Sum("dp", mx_part, mixing, d2)
+    parts(po, 0, keeps, 0, 2)
+    open_ring(2)
+    complete(2, 1, NZ)
+    sum_d.drain()
+    fo_part[...] = dot_tn(attn[...], cg[...]).astype(BF)
+    sum_d2 = Sum("dp", fo_part, mixing, d2)
     sum_d2.first()
-    parts(po, 0, keeps, 0, 4)
+    parts(po, 0, keeps, 2, 5)
     sum_t2.second()
     ring(2, 2)
-    parts(po, 0, keeps, 4, NQ)
+    parts(po, 0, keeps, 5, NQ)
     contribute(0)
-    complete(0)
-    ring(0, 1)
+    open_ring(0)
+    complete(0, 1, NZ)
     ring(2, 3)
-    sum_t2.third()
 
     @pl.when(keeps)
     def _():
         y_second()
 
+    sum_t2.third()
     contribute(1)
+    open_ring(1)
     ring(0, 2)
-    swap_grad(1).wait_recv()
     turn(1, qo)
     parts(px, 1, away, 0, 4)
+    complete(1, 1, NZ)
     ring(2, 4)
-    sum_t2.across()
     parts(px, 1, away, 4, NQ)
     ring(0, 3)
-    complete(1)
-    ring(1, 1)
+    ring(1, 2)
+
+    @pl.when(away)
+    def _():
+        y_second()
 
     @pl.when(keeps)
     def _():
         y_third()
 
+    sum_t2.across()
+    sum_d2.second()
+    ring(2, 5)
+    ring(0, 4)
+
     @pl.when(away)
     def _():
-        y_second()
-
-    sum_d2.second()
-    ring(2, 5)
-    ring(1, 2)
-    ring(0, 4)
-    sum_t2.fourth()
+        y_home()
 
     @pl.when(keeps)
     def _():
         x_last()
 
+    ring(1, 3)
+    sum_t2.fourth()
+    sum_d2.third()
+    ring(0, 5)
+
     @pl.when(away)
     def _():
-        y_third()
-
-    ring(1, 3)
-    sum_d2.third()
-    ring(0, 5)
-    home = remote(fs, fv, fs_ss, fs_rs, dp=other, tensor=sibling)
-
-    @pl.when(away)
-    def _():
-        x_last()
-        fs[...] = ng[...].astype(BF)
-        home.start()
-
-    ring(1, 4)
-    sum_d2.fourth()
-
-    @pl.when(away)
-    def _():
-        home.wait_recv()
-        ng[...] = fv[...].astype(F32)
+        for which in range(2):
+            home(which).wait_recv()
+        ng[...] = fv[0].astype(F32) + fv[1].astype(F32)
 
     grad = ng[...]
-    scaled = grad * gcol[mine_rows, 0:1]
+    scaled = grad * gcol[:, 0:1]
     lt[tensor, 0:1, :] = jnp.sum(scaled, axis=0, keepdims=True)
     lt[tensor, 1:2, :] = jnp.sum(scaled * hat[...], axis=0, keepdims=True)
     slot = lt.at[tensor]
@@ -658,6 +702,7 @@
     slot = gs.at[dp]
     for k in range(1, NR):
         go(remote(slot, slot, gs_ss.at[k], gs_rs.at[k], dp=rem(dp + k, NR)))
+    ring(1, 4)
     sum_t2.last()
     ro_t[...] = (xt[mine_rows, :].astype(F32) + dot_nt(dect[...], code[...])).astype(BF)
 
@@ -666,8 +711,9 @@
         remote(slot, slot, lt_ss.at[k], lt_rs.at[k], tensor=tensor).wait_recv()
     sums = jnp.sum(lt[...], axis=0)
     lead, trail = sums[0:1, :] * (1.0 / D), sums[1:2, :] * (1.0 / D)
-    scaled = ng[...] * gcol[mine_rows, 0:1]
+    scaled = ng[...] * gcol[:, 0:1]
     gi_t[...] = (got[...].astype(F32) + st[0:1, :] * (scaled - lead - hat[...] * trail)).astype(BF)
+    sum_d2.fourth()
     ring(1, 5)
     sum_d2.last()
     gow_t[...] = dot_nt(enc[...], mixing[...]) * (1.0 / NR)
@@ -676,15 +722,19 @@
         remote(slot, slot, gs_ss.at[k], gs_rs.at[k], dp=dp).wait_recv()
     gb[...] = jnp.sum(gs[...], axis=0) * (1.0 / NR)
 
-    for total in (sum_t, sum_d, sum_t2, sum_d2):
+    for total in (sum_t2, sum_d2):
         total.drain()
-    swap.wait_send()
     for copy in sent:
         copy.wait_send()
 
-    @pl.when(jnp.logical_not(keeps))
+    @pl.when(keeps)
     def _():
-        home.wait_send()
+        swap.wait_send()
+
+    @pl.when(away)
+    def _():
+        for which in range(2):
+            home(which).wait_send()
 
     @pl.loop(0, NQ)
     def _(i):
@@ -708,17 +758,17 @@
     far = pl.BlockSpec(memory_space=pl.ANY)
     scratch = [
         v(BF, SEQ, D), v(BF, 3, NZ * BLK, 256), v(BF, 2, NZ, BLK, SEQ), v(BF, NZ, BLK, SEQ), v(F32, 2, W3, SEQ),
-        v(F32, SEQ, 128), v(F32, SEQ, 128), v(BF, SLAB, SEQ), v(F32, SLAB, 128), v(F32, BLK, SEQ), v(F32, 8, SEQ),
-        v(BF, SEQ, C), v(BF, 256, C), v(BF, SEQ, C), v(BF, 256, C), v(BF, W3, SEQ), v(BF, W3, SEQ), v(BF, W3, SEQ),
+        v(F32, SEQ, 128), v(F32, SEQ, 128), v(BF, SLAB, SEQ), v(F32, BLK, 128), v(F32, BLK, SEQ), v(F32, 8, SEQ),
+        v(BF, SEQ, C), v(BF, 256, C), v(BF, SEQ, C), v(BF, 256, C), v(BF, W3, SEQ), v(BF, W3, SEQ),
         v(BF, SEQ, W3), v(BF, SEQ, 256), v(BF, SEQ, 256), v(BF, SEQ, W3), v(BF, SEQ, W3), v(BF, 2, W3, SEQ),
-        v(F32, SEQ, 512), v(F32, 2, SEQ, SEQ),
+        v(F32, SEQ, 512),
         v(BF, NZ, 3, BLK, 256), v(BF, 3, 2, HB, 256), v(BF, 3, 2, 3, BLK, 256),
         v(BF, NQ, BLK, SEQ), v(BF, NQ, BLK, SEQ), v(BF, NQ, BLK, SEQ), v(BF, NQ, BLK, SEQ), v(BF, 2, 2, HB, SEQ), v(BF, 2, 2, BLK, SEQ),
-        v(BF, BLK, SEQ), v(BF, BLK, SEQ), v(BF, BLK, SEQ), v(BF, BLK, SEQ), v(F32, BLK, SEQ),
-        v(F32, NR, 8, SEQ), v(F32, NR, 8, 384), v(BF, SEQ, C), v(BF, 256, C), v(BF, SEQ, C), v(BF, 256, C),
+        v(BF, 2, BLK, SEQ), v(BF, 2, BLK, SEQ), v(F32, BLK, SEQ),
+        v(F32, NR, 8, SEQ), v(F32, NR, 8, 384), v(BF, SEQ, C), v(BF, 256, C),
         sum_buffers(SEQ, NY), sum_buffers(256, NZ), sum_buffers(SEQ, NY), sum_buffers(256, NZ),
-        dma(4), one, dma(2, 3, 4), dma(2, 3, 4), dma(4, 4), dma(4, 4), dma(4, 4), dma(4, 4), dma(3), dma(3), dma(3), dma(3),
-        dma(3, 2), dma(3, 2), dma(3, 2, 3), dma(3, 2, 3), dma(NQ), dma(NQ), dma(2, 2), dma(2, 2), dma(2, 2), dma(2, 2), one, one, one, one,
+        dma(4), one, dma(2, 3, 4), dma(2, 3, 4), dma(4), dma(4), dma(3, 4), dma(3, 4), dma(4, 4), dma(4, 4), dma(3), dma(3), dma(3), dma(3),
+        dma(3, 2), dma(3, 2), dma(3, 2, 3), dma(3, 2, 3), dma(NQ), dma(NQ), dma(2, 2), dma(2, 2), dma(2, 2), dma(2, 2), one, one, dma(2), dma(2),
         dma(NR), dma(NR), dma(NR), dma(NR),
     ]
     return pl.pallas_call(

time: 156 us -> 152 us (0.974)
  Pallas kernels: 153 us -> 150 us
    pallas_call x1, Pallas kernels: 151 us -> 148 us  [sublayer(): pl.pallas_call(kernel, out_shape=[shape((BLK, SEQ), BF), shape((BLK, SEQ)...]
where the time goes in v6:
time: 152 us
  Pallas kernels  150 us (99%)
    pallas_call x1, Pallas kernels, sublayer(): pl.pallas_call(kernel, out_shape=[shape((BLK, SEQ), BF), shape((BLK, SEQ)...  148 us

profile of v6, /device:TPU:1, one launch (start us, length us, event | category | flops | bytes accessed | tf_op | source)
XLA Modules:
  0.0 152.3 jit_solution(13897021070788255624)
XLA Ops:
  0.6 147.5 %shard_map.127 = (bf16[320,512]{1,0:T(8,128)(2,1)}, bf16[320,512]{1,0:T(8,128)(2,1)}, f32[3,320,256]{2,1,0:T(8,128)}, f32[320,256]{1,0:T(8,128)}, f32[8,384]{1,0:T(8,128)}) custom-call(bf16[512,5120]{1,0:T(8,128)(2,1)} %x_hbm.1, f32[1,5120]{1,0:T(1,128)} %bitcast.11, f32[1,5120]{1,0:T(1,128)} %bitcast.12, bf16[3,320,256]{2,1,0:T(8,128)(2,1)} %w_in.1, ...), custom_call_target="tpu_custom_call" | custom-call | tf_op jit(solution)/shard_map/pallas_call | solution.py:774
  148.1 2.8 %shard_map.128 = (bf16[320,512]{1,0:T(8,128)(2,1)}, bf16[320,512]{1,0:T(8,128)(2,1)}, f32[3,320,256]{2,1,0:T(8,128)}, f32[320,256]{1,0:T(8,128)}) custom-call(bf16[320,512]{1,0:T(8,128)(2,1)} %get-tuple-element.15.refs_0_, bf16[320,512]{1,0:T(8,128)(2,1)} %get-tuple-element.16.refs_1_, f32[3,320,256]{2,1,0:T(8,128)} %get-tuple-element.17.refs_2_, ...), custom_call_target="tpu_custom_call" | custom-call | tf_op jit(solution)/shard_map/pallas_call | solution.py:804
  150.9 1.4 slice_reduce_fusion

commit v7 on v6

--- a/solution.py
+++ b/solution.py
@@ -623,47 +623,55 @@
     parts(po, 0, keeps, 0, 2)
     open_ring(2)
     complete(2, 1, NZ)
+    sum_t2.second()
     sum_d.drain()
     fo_part[...] = dot_tn(attn[...], cg[...]).astype(BF)
     sum_d2 = Sum("dp", fo_part, mixing, d2)
     sum_d2.first()
-    parts(po, 0, keeps, 2, 5)
-    sum_t2.second()
+    parts(po, 0, keeps, 2, 4)
     ring(2, 2)
-    parts(po, 0, keeps, 5, NQ)
+    sum_t2.third()
+    parts(po, 0, keeps, 4, 6)
     contribute(0)
     open_ring(0)
+    parts(po, 0, keeps, 6, NQ)
     complete(0, 1, NZ)
     ring(2, 3)
-
-    @pl.when(keeps)
-    def _():
-        y_second()
-
-    sum_t2.third()
+    sum_t2.across()
     contribute(1)
     open_ring(1)
     ring(0, 2)
     turn(1, qo)
-    parts(px, 1, away, 0, 4)
+    parts(px, 1, away, 0, 2)
+
+    @pl.when(keeps)
+    def _():
+        y_second()
+
+    ring(2, 4)
     complete(1, 1, NZ)
-    ring(2, 4)
-    parts(px, 1, away, 4, NQ)
+    parts(px, 1, away, 2, 4)
     ring(0, 3)
+    sum_t2.fourth()
+    parts(px, 1, away, 4, 6)
     ring(1, 2)
+    ring(2, 5)
+    parts(px, 1, away, 6, NQ)
 
     @pl.when(away)
     def _():
         y_second()
 
+    ring(0, 4)
+    sum_d2.second()
+    ring(1, 3)
+
     @pl.when(keeps)
     def _():
         y_third()
 
-    sum_t2.across()
-    sum_d2.second()
-    ring(2, 5)
-    ring(0, 4)
+    ring(0, 5)
+    ring(1, 4)
 
     @pl.when(away)
     def _():
@@ -673,10 +681,8 @@
     def _():
         x_last()
 
-    ring(1, 3)
-    sum_t2.fourth()
     sum_d2.third()
-    ring(0, 5)
+    ring(1, 5)
 
     @pl.when(away)
     def _():
@@ -702,7 +708,7 @@
     slot = gs.at[dp]
     for k in range(1, NR):
         go(remote(slot, slot, gs_ss.at[k], gs_rs.at[k], dp=rem(dp + k, NR)))
-    ring(1, 4)
+    sum_d2.fourth()
     sum_t2.last()
     ro_t[...] = (xt[mine_rows, :].astype(F32) + dot_nt(dect[...], code[...])).astype(BF)
 
@@ -713,8 +719,6 @@
     lead, trail = sums[0:1, :] * (1.0 / D), sums[1:2, :] * (1.0 / D)
     scaled = ng[...] * gcol[:, 0:1]
     gi_t[...] = (got[...].astype(F32) + st[0:1, :] * (scaled - lead - hat[...] * trail)).astype(BF)
-    sum_d2.fourth()
-    ring(1, 5)
     sum_d2.last()
     gow_t[...] = dot_nt(enc[...], mixing[...]) * (1.0 / NR)
     for k in range(1, NR):

time: 152 us -> 164 us (1.079)
  Pallas kernels: 150 us -> 162 us
    pallas_call x1, Pallas kernels: 148 us -> 159 us  [sublayer(): pl.pallas_call(kernel, out_shape=[shape((BLK, SEQ), BF), shape((BLK, SEQ)...]
where the time goes in v7:
time: 164 us
  Pallas kernels  162 us (99%)
    pallas_call x1, Pallas kernels, sublayer(): pl.pallas_call(kernel, out_shape=[shape((BLK, SEQ), BF), shape((BLK, SEQ)...  159 us

profile of v7, /device:TPU:1, one launch (start us, length us, event | category | flops | bytes accessed | tf_op | source)
XLA Modules:
  0.0 163.8 jit_solution(2195589876873735733)
XLA Ops:
  0.6 159.0 %shard_map.127 = (bf16[320,512]{1,0:T(8,128)(2,1)}, bf16[320,512]{1,0:T(8,128)(2,1)}, f32[3,320,256]{2,1,0:T(8,128)}, f32[320,256]{1,0:T(8,128)}, f32[8,384]{1,0:T(8,128)}) custom-call(bf16[512,5120]{1,0:T(8,128)(2,1)} %x_hbm.1, f32[1,5120]{1,0:T(1,128)} %bitcast.11, f32[1,5120]{1,0:T(1,128)} %bitcast.12, bf16[3,320,256]{2,1,0:T(8,128)(2,1)} %w_in.1, ...), custom_call_target="tpu_custom_call" | custom-call | tf_op jit(solution)/shard_map/pallas_call | solution.py:778
  159.6 2.8 %shard_map.128 = (bf16[320,512]{1,0:T(8,128)(2,1)}, bf16[320,512]{1,0:T(8,128)(2,1)}, f32[3,320,256]{2,1,0:T(8,128)}, f32[320,256]{1,0:T(8,128)}) custom-call(bf16[320,512]{1,0:T(8,128)(2,1)} %get-tuple-element.15.refs_0_, bf16[320,512]{1,0:T(8,128)(2,1)} %get-tuple-element.16.refs_1_, f32[3,320,256]{2,1,0:T(8,128)} %get-tuple-element.17.refs_2_, ...), custom_call_target="tpu_custom_call" | custom-call | tf_op jit(solution)/shard_map/pallas_call | solution.py:808
  162.4 1.4 slice_reduce_fusion

commit v8 on v6

--- a/solution.py
+++ b/solution.py
@@ -703,6 +703,7 @@
     for k in range(1, NR):
         go(remote(slot, slot, gs_ss.at[k], gs_rs.at[k], dp=rem(dp + k, NR)))
     ring(1, 4)
+    sum_d2.fourth()
     sum_t2.last()
     ro_t[...] = (xt[mine_rows, :].astype(F32) + dot_nt(dect[...], code[...])).astype(BF)
 
@@ -713,7 +714,6 @@
     lead, trail = sums[0:1, :] * (1.0 / D), sums[1:2, :] * (1.0 / D)
     scaled = ng[...] * gcol[:, 0:1]
     gi_t[...] = (got[...].astype(F32) + st[0:1, :] * (scaled - lead - hat[...] * trail)).astype(BF)
-    sum_d2.fourth()
     ring(1, 5)
     sum_d2.last()
     gow_t[...] = dot_nt(enc[...], mixing[...]) * (1.0 / NR)

time: 152 us -> 152 us (level)
  no operation moved by 1% of the time
where the time goes in v8:
time: 152 us
  Pallas kernels  150 us (99%)
    pallas_call x1, Pallas kernels, sublayer(): pl.pallas_call(kernel, out_shape=[shape((BLK, SEQ), BF), shape((BLK, SEQ)...  148 us

profile of v8, /device:TPU:1, one launch (start us, length us, event | category | flops | bytes accessed | tf_op | source)
XLA Modules:
  0.0 152.3 jit_solution(16630857004557997936)
XLA Ops:
  0.6 147.5 %shard_map.127 = (bf16[320,512]{1,0:T(8,128)(2,1)}, bf16[320,512]{1,0:T(8,128)(2,1)}, f32[3,320,256]{2,1,0:T(8,128)}, f32[320,256]{1,0:T(8,128)}, f32[8,384]{1,0:T(8,128)}) custom-call(bf16[512,5120]{1,0:T(8,128)(2,1)} %x_hbm.1, f32[1,5120]{1,0:T(1,128)} %bitcast.11, f32[1,5120]{1,0:T(1,128)} %bitcast.12, bf16[3,320,256]{2,1,0:T(8,128)(2,1)} %w_in.1, ...), custom_call_target="tpu_custom_call" | custom-call | tf_op jit(solution)/shard_map/pallas_call | solution.py:774
  148.1 2.8 %shard_map.128 = (bf16[320,512]{1,0:T(8,128)(2,1)}, bf16[320,512]{1,0:T(8,128)(2,1)}, f32[3,320,256]{2,1,0:T(8,128)}, f32[320,256]{1,0:T(8,128)}) custom-call(bf16[320,512]{1,0:T(8,128)(2,1)} %get-tuple-element.15.refs_0_, bf16[320,512]{1,0:T(8,128)(2,1)} %get-tuple-element.16.refs_1_, f32[3,320,256]{2,1,0:T(8,128)} %get-tuple-element.17.refs_2_, ...), custom_call_target="tpu_custom_call" | custom-call | tf_op jit(solution)/shard_map/pallas_call | solution.py:804
  150.9 1.4 slice_reduce_fusion
